TPU v7x, 256 devices: a whole 4x4x8 slice. The times are simulated.
256 devices in a mesh: ep: 32 (over z, x), etp: 8 (over y, core).
Axes of the slice: x: 4, y: 4, z: 8, core: 2. Of those that a mesh axis runs over, the one named last changes fastest.
Arguments:
- tokens: bfloat16 [8192, 5120], P('ep', 'etp'), may hold values from -6 to 6
- routes: int32 [8192, 1], P('ep'), may hold values from 0 to 15; in each aligned block of 256 rows (0 to 255, 256 to 511, ...) at most 24 rows name the same one
- router_gate: bfloat16 [8192, 1], P('ep'), may hold values from 0.19921875 to 1
- w_gate: bfloat16 [5120, 65536], P(None, ('ep', 'etp')), may hold values from -0.078125 to 0.078125
- w_up: bfloat16 [5120, 65536], P(None, ('ep', 'etp')), may hold values from -0.078125 to 0.078125
- w_down: bfloat16 [65536, 5120], P(('ep', 'etp')), may hold values from -0.375 to 0.375
Outputs:
- moe_out: bfloat16 [8192, 5120], P('ep', 'etp')
Inputs may be any that keep to these rules, and one draw needn't show every extreme that they name: `routes`: in the rows of one index of ep no expert is named more than 24 times, and in every draw some expert is named exactly 24 times by some index's rows; every expert is named by some token.
All inputs are finite; a program needn't handle non-finite values.
Results may differ from a plain program's by a relative error of at most 0.019.
Values may be sent and summed in bfloat16 or wider, within the bound.
A program may use at most 128 MiB of HBM per device.

v0:
```python
import jax
import jax.numpy as jnp
from jax import lax
from jax.sharding import PartitionSpec as P


def on_device(tokens, routes, router_gate, w_gate, w_up, w_down):
    tok_dev = tokens.shape[0]
    ep_count = lax.axis_size("ep")
    etp_count = lax.axis_size("etp")
    experts = ep_count // 2
    capacity = 3 * tok_dev // ep_count
    feat_local = w_down.shape[1] // etp_count
    expert_of = routes[:, 0]
    onehot = (expert_of[:, None] == jnp.arange(experts, dtype=jnp.int32)[None, :]).astype(jnp.int32)
    earlier = jnp.cumsum(onehot, axis=0) - onehot
    slot_of = expert_of * capacity + jnp.sum(earlier * onehot, axis=1)
    dispatch_map = slot_of[None, :] == jnp.arange(experts * capacity, dtype=jnp.int32)[:, None]
    feat_width = tokens.shape[1]
    outgoing = jnp.dot(
        dispatch_map.astype(jnp.bfloat16), tokens, preferred_element_type=jnp.float32
    ).astype(jnp.bfloat16)
    doubled = jnp.broadcast_to(
        outgoing.reshape(experts, 1, capacity, feat_width), (experts, 2, capacity, feat_width)
    ).reshape(ep_count, capacity, feat_width)
    arrived = lax.all_to_all(doubled, "ep", split_axis=0, concat_axis=0, tiled=True)
    received = arrived.reshape(ep_count * capacity, feat_width)
    shard_piece = lax.all_gather(received, "etp", axis=1, tiled=True)
    gate_pre = jnp.dot(shard_piece, w_gate, preferred_element_type=jnp.float32)
    up_pre = jnp.dot(shard_piece, w_up, preferred_element_type=jnp.float32)
    hidden = (jax.nn.silu(gate_pre) * up_pre).astype(jnp.bfloat16)
    partial_out = lax.dot_general(
        w_down, hidden, (((0,), (1,)), ((), ())), preferred_element_type=jnp.float32
    )
    summed = lax.psum_scatter(
        lax.optimization_barrier(partial_out.astype(jnp.bfloat16))
        .astype(jnp.float32)
        .astype(jnp.bfloat16),
        "etp",
        scatter_dimension=0,
        tiled=True,
    ).astype(jnp.float32)
    returned = lax.all_to_all(
        summed.reshape(feat_local, ep_count, capacity).astype(jnp.bfloat16),
        "ep",
        split_axis=1,
        concat_axis=1,
        tiled=True,
    ).astype(jnp.float32)
    merged = jnp.sum(returned.reshape(feat_local, experts, 2, capacity), axis=2)
    merged = merged.reshape(feat_local, experts * capacity)
    combined = lax.dot_general(
        dispatch_map.astype(jnp.float32),
        merged,
        (((0,), (1,)), ((), ())),
        precision=lax.Precision.HIGHEST,
        preferred_element_type=jnp.float32,
    )
    return (combined * router_gate.astype(jnp.float32)).astype(jnp.bfloat16)


def solution(mesh):
    return jax.shard_map(
        on_device,
        mesh=mesh,
        in_specs=(
            P("ep", "etp"),
            P("ep", None),
            P("ep", None),
            P(None, ("ep", "etp")),
            P(None, ("ep", "etp")),
            P(("ep", "etp"), None),
        ),
        out_specs=P("ep", "etp"),
        check_vma=False,
    )
```

profile of v0, /device:TPU:32, one launch (start us, length us, event | category | flops | bytes accessed | tf_op | source)
XLA Modules:
  0.0 230.1 jit_solution(798198930486027261)
XLA Ops:
  6.5 0.0 copy-start
  6.5 0.0 all-gather.2.cloned.1.call-start
  6.5 0.8 fusion.14
  7.4 0.6 reduce-window.6
  7.9 0.2 slice_reduce_fusion
  8.2 0.8 fusion.13
  8.9 0.7 multiply_add_fusion
  9.6 1.3 convolution_convert_fusion.1
  10.9 0.1 broadcast_in_dim.5
  11.0 37.1 %all_to_all.10 = bf16[32,24,640]{2,1,0:T(8,128)(2,1)} all-to-all(bf16[32,24,640]{2,1,0:T(8,128)(2,1)S(1)} %bitcast.43), channel_id=1, replica_groups=mesh['ep'=32,'etp'=8] {'ep'}, dimensions={0} | all-to-all | bytes 1966080 | tf_op jit(solution)/shard_map/all_to_all | solution.py:26
  48.1 0.0 all-gather.2.cloned.1.call-update
  48.2 0.0 reduce-scatter.4.cloned.1.call-start
  48.2 47.8 %all-gather.2.cloned.1.call-done = bf16[768,5120]{1,0:T(8,128)(2,1)} async-done(((bf16[768,640]{1,0:T(8,128)(2,1)}), bf16[768,5120]{1,0:T(8,128)(2,1)}) %all-gather.2.cloned.1.call-update) | async-done | bytes 7864336 | tf_op jit(solution)/shard_map/all_gather | solution.py:28
  96.0 6.2 %fusion.16 = f32[768,256]{1,0:T(8,128)S(1)} fusion(bf16[768,5120]{1,0:T(8,128)(2,1)} %all-gather.2.cloned.1.call-done, bf16[5120,256]{1,0:T(8,128)(2,1)} %param.9), kind=kOutput, calls=%fused_computation.28 | convolution fusion | flops 2013265920 | bytes 11272192 | tf_op jit(solution)/shard_map/dot_general | solution.py:29
  102.1 0.0 copy-done
  102.2 16.4 %fusion = bf16[5120,768]{0,1:T(8,128)(2,1)} fusion(bf16[256,5120]{1,0:T(8,128)(2,1)S(1)} %copy-done, bf16[768,5120]{1,0:T(8,128)(2,1)} %all-gather.2.cloned.1.call-done, bf16[5120,256]{1,0:T(8,128)(2,1)} %param.10, f32[768,256]{1,0:T(8,128)S(1)} %fusion.16), kind=kOutput, calls=%fused_computation.1 | convolution fusion | flops 4031643648 | bytes 21757952 | tf_op jit(solution)/shard_map/dot_general | solution.py:32
  118.6 10.6 %copy.9 = bf16[5120,768]{1,0:T(8,128)(2,1)} copy(bf16[5120,768]{0,1:T(8,128)(2,1)} %fusion) | data formatting | bytes 15728640
  129.2 0.0 reduce-scatter.4.cloned.1.call-update
  129.2 0.0 copy-start.1
  129.2 52.9 %reduce-scatter.4.cloned.1.call-done = bf16[640,768]{1,0:T(8,128)(2,1)} async-done(((bf16[5120,768]{1,0:T(8,128)(2,1)}), bf16[640,768]{1,0:T(8,128)(2,1)}) %reduce-scatter.4.cloned.1.call-update) | async-done | bytes 983056
  182.1 2.2 copy.10
  184.3 10.1 %all-to-all-start.1 = ((bf16[640,32,24]{0,2,1:T(8,128)(2,1)}), bf16[640,32,24]{0,2,1:T(8,128)(2,1)}, u32[]{:S(2)}, u32[]{:S(2)}) async-start(bf16[640,32,24]{0,2,1:T(8,128)(2,1)} %bitcast.41), calls=%async_computation.1 | async-start | bytes 1966080 | tf_op jit(solution)/shard_map/all_to_all | solution.py:43
  194.4 0.0 copy-done.1
  194.4 25.7 %all-to-all-done.1 = bf16[640,32,24]{0,2,1:T(8,128)(2,1)} async-done(((bf16[640,32,24]{0,2,1:T(8,128)(2,1)}), bf16[640,32,24]{0,2,1:T(8,128)(2,1)}, u32[]{:S(2)}, u32[]{:S(2)}) %all-to-all-start.1) | async-done | bytes 983072 | tf_op jit(solution)/shard_map/all_to_all | solution.py:43
  220.2 1.5 convert_reduce_fusion
  221.7 1.6 fusion.2
  (3 shorter events, 0.0 us)
Async XLA Ops:
  6.5 95.6 %copy-start = (bf16[256,5120]{1,0:T(8,128)(2,1)S(1)}, bf16[256,5120]{1,0:T(8,128)(2,1)}, u32[]{:S(2)}) copy-start(bf16[256,5120]{1,0:T(8,128)(2,1)} %param.11) | copy-start | bytes 7864324
  6.5 89.4 %all-gather.2.cloned.1.call-start = ((), (), s32[]{:S(2)}) async-start(), calls=%async_computation.3 | async-start | bytes 8847360 | tf_op jit(solution)/shard_map/all_gather | solution.py:28
  48.2 133.9 %reduce-scatter.4.cloned.1.call-start = ((), (), s32[]{:S(2)}) async-start(), calls=%async_computation.4 | async-start | bytes 8847360
  129.2 65.2 %copy-start.1 = (bf16[256,1]{0,1:T(2,128)(2,1)S(1)}, bf16[256,1]{0,1:T(2,128)(2,1)}, u32[]{:S(2)}) copy-start(bf16[256,1]{0,1:T(2,128)(2,1)} %param.8) | copy-start | bytes 1540
  184.3 35.9 %all-to-all-start.1 = ((bf16[640,32,24]{0,2,1:T(8,128)(2,1)}), bf16[640,32,24]{0,2,1:T(8,128)(2,1)}, u32[]{:S(2)}, u32[]{:S(2)}) async-start(bf16[640,32,24]{0,2,1:T(8,128)(2,1)} %bitcast.41), calls=%async_computation.1 | async-start | bytes 1966080 | tf_op jit(solution)/shard_map/all_to_all | solution.py:43
Sparse Core Ops, SparseCore 0:
  48.3 47.6 all-gather.1
  129.3 52.7 reduce-scatter.3
where the time goes:
time: 231 us; the launch traced here: 230 us
  waiting for transfers between devices  126 us (55%)
  blocking collectives  37.1 us (16%)
  matrix products  25.4 us (11%)
  between operations  13.5 us (6%)
  local copies, waits for them, and re-layouts  13.1 us (6%)
  starting transfers between devices  10.1 us (4%)
  other arithmetic  4.37 us (2%)
    unnamed x3, waiting for transfers between devices  52.9 us
    all_gather x1, waiting for transfers between devices, on_device(): shard_piece = lax.all_gather(received, 'etp', axis=1, tiled=True)  47.8 us
    all_to_all x1, blocking collectives, on_device(): lax.all_to_all(doubled, 'ep', split_axis=0, concat_axis=0, tiled=True)  37.1 us
    all_to_all x1, waiting for transfers between devices, on_device(): lax.all_to_all(summed.reshape(feat_local, ep_count, capacity).astype(jnp....  25.7 us
    dot_general x1, matrix products, on_device(): lax.dot_general(w_down, hidden, (((0,), (1,)), ((), ())), preferred_eleme...  16.4 us
    unnamed x6, local copies, waits for them, and re-layouts  12.9 us
    all_to_all x1, starting transfers between devices, on_device(): lax.all_to_all(summed.reshape(feat_local, ep_count, capacity).astype(jnp....  10.1 us
    dot_general x1, matrix products, on_device(): gate_pre = jnp.dot(shard_piece, w_gate, preferred_element_type=jnp.float32)  6.17 us
  transfers between devices with their start and end apart: 3, of which 3 were waited for; matrix products, arithmetic and copies ran while one was open for 0% of the time, Pallas kernels for 0%

commit v1 on v0

v1 whole, which is shorter than its diff:
```python
import functools

import jax
import jax.numpy as jnp
from jax import lax
from jax.experimental import pallas as pl
from jax.experimental.pallas import tpu as pltpu
from jax.sharding import PartitionSpec as P

MESH = pl.DeviceIdType.MESH
F32 = jnp.float32
BF16 = jnp.bfloat16

CHUNKS = ((0, 1), (7, 2), (6, 3), (5, 4))
NC = len(CHUNKS)


def kernel(sizes, tokens, routes, gate, w_gate, w_up, w_down, out,
           w_gu, w_dn, slots, outgo, zrecv, cross, xs, acc, parts, crecv,
           ring2, ring2_in, ring_up, ring_up_in, ring_dn, ring_dn_in,
           own, xn_out, xn_in, fin, xc_in, rets, retr,
           w_sem, send_sem, recv_sem):
    nx, ny, nz, cap, feat = sizes
    half = 4 * cap
    ep = lax.axis_index("ep")
    etp = lax.axis_index("etp")
    z, x = ep // nx, ep % nx
    y, c = etp // 2, etp % 2

    def at(zz, xx, yy, cc):
        return {"ep": zz * nx + xx, "etp": yy * 2 + cc}

    y_up, y_dn = at(z, x, (y + 1) % ny, c), at(z, x, (y + ny - 1) % ny, c)
    core = at(z, x, y, 1 - c)
    x_near = at(z, x + 1 - 2 * (x % 2), y, c)
    x_cross = at(z, nx - 1 - x, y, c)

    barrier = pltpu.get_barrier_semaphore()
    peers = [y_up, y_dn, core, x_near, x_cross] + [
        at((z + j) % nz, x, y, c) for j in range(1, nz)
    ]
    for peer in peers:
        pl.semaphore_signal(barrier, inc=1, device_id=peer, device_id_type=MESH)

    loads = []
    for r in range(ny):
        for k in range(2):
            shard = (((y + r) % ny) * 2 + (c + k) % 2) * feat
            shard = pl.multiple_of(shard, 128)
            into = pl.ds(k * feat, feat)
            unit = w_gate.shape[1]
            loads.append((w_gate.at[pl.ds(shard, feat), :], w_gu.at[r, into, pl.ds(0, unit)]))
            loads.append((w_up.at[pl.ds(shard, feat), :], w_gu.at[r, into, pl.ds(unit, unit)]))
            loads.append((w_down.at[:, pl.ds(shard, feat)], w_dn.at[r, :, into]))
    loads = [pltpu.make_async_copy(a, b, w_sem.at[i]) for i, (a, b) in enumerate(loads)]
    for load in loads:
        load.start()

    rows = routes.shape[0]
    expert = routes[...]
    lane = lax.broadcasted_iota(jnp.int32, (rows, 128), 1)
    onehot = (expert == lane).astype(F32)
    before = lax.broadcasted_iota(jnp.int32, (rows, rows), 1) < lax.broadcasted_iota(
        jnp.int32, (rows, rows), 0
    )
    ranks = jnp.dot(before.astype(F32).astype(BF16), onehot.astype(BF16), preferred_element_type=F32)
    rank = jnp.sum(ranks * onehot, axis=1, keepdims=True).astype(jnp.int32)
    unit_of = (z + nz - (expert >> 1)) & (nz - 1)
    other = (expert & 1) != x // 2
    slot = unit_of * (2 * cap) + jnp.where(other, cap, 0) + rank
    place = lax.broadcasted_iota(jnp.int32, (rows, nz * 2 * cap), 1)
    slots[...] = (slot == place).astype(F32).astype(BF16)
    sent = lax.dot_general(
        slots[...], tokens[...], (((0,), (0,)), ((), ())), preferred_element_type=F32
    )
    outgo[...] = sent.astype(BF16).reshape(nz, 2 * cap, feat)

    started = []
    used = [0]

    def send(src, dst, device):
        i = used[0]
        used[0] += 1
        copy = pltpu.make_async_remote_copy(
            src_ref=src, dst_ref=dst, send_sem=send_sem.at[i], recv_sem=recv_sem.at[i],
            device_id=device, device_id_type=MESH,
        )
        copy.start()
        started.append(copy)
        return copy

    pl.semaphore_wait(barrier, len(peers))

    z_copy = {}
    for pair in CHUNKS:
        for j in pair:
            if j:
                z_copy[j] = send(outgo.at[j], zrecv.at[j], at((z + nz - j) % nz, x, y, c))

    MINE, THEIRS = pl.ds(0, feat), pl.ds(feat, feat)
    LOW, HIGH = pl.ds(0, half), pl.ds(half, half)
    copies = [dict() for _ in CHUNKS]

    def unit_block(j):
        if j:
            z_copy[j].wait_recv()
            return zrecv[j].astype(F32)
        return outgo[j].astype(F32)

    def d1(k):
        first, second = (unit_block(j) for j in CHUNKS[k])
        xs[k, 0, : half // 2, :feat] = jnp.concatenate([first[:cap], second[:cap]], axis=0).astype(BF16)
        cross[k] = jnp.concatenate([first[cap:], second[cap:]], axis=0).astype(BF16)
        copies[k]["cross"] = send(
            cross.at[k], xs.at[k, 0, pl.ds(half // 2, half // 2), MINE], x_cross
        )

    def d2(k):
        co = copies[k]
        co["cross"].wait_recv()
        mine = xs.at[k, 0, LOW, MINE]
        co["xn"] = send(mine, xs.at[k, 0, HIGH, MINE], x_near)
        co["up_low"] = send(mine, xs.at[k, 3, LOW, MINE], y_up)
        co["dn_low"] = send(mine, xs.at[k, 1, LOW, MINE], y_dn)
        co["c0_low"] = send(mine, xs.at[k, 0, LOW, THEIRS], core)

    def d3(k):
        co = copies[k]
        co["xn"].wait_recv()
        mine = xs.at[k, 0, HIGH, MINE]
        co["dn_high"] = send(mine, xs.at[k, 1, HIGH, MINE], y_dn)
        co["up_high"] = send(mine, xs.at[k, 3, HIGH, MINE], y_up)
        co["c0_high"] = send(mine, xs.at[k, 0, HIGH, THEIRS], core)

    def d4(k):
        co = copies[k]
        co["up_low"].wait_recv()
        co["f_up"] = send(xs.at[k, 3, LOW, MINE], xs.at[k, 2, LOW, MINE], y_up)
        co["dn_high"].wait_recv()
        co["f_dn"] = send(xs.at[k, 1, HIGH, MINE], xs.at[k, 2, HIGH, MINE], y_dn)
        co["dn_low"].wait_recv()
        co["up_high"].wait_recv()
        co["c1"] = send(xs.at[k, 1, :, MINE], xs.at[k, 1, :, THEIRS], core)
        co["c3"] = send(xs.at[k, 3, :, MINE], xs.at[k, 3, :, THEIRS], core)

    def d5(k):
        co = copies[k]
        co["f_up"].wait_recv()
        co["f_dn"].wait_recv()
        co["c2"] = send(xs.at[k, 2, :, MINE], xs.at[k, 2, :, THEIRS], core)

    def compute(k):
        co = copies[k]
        if k == 0:
            for load in loads:
                load.wait()
        co["c0_low"].wait_recv()
        co["c0_high"].wait_recv()
        acc[...] = jnp.dot(xs[k, 0], w_gu[0], preferred_element_type=F32)
        co["c1"].wait_recv()
        acc[...] += jnp.dot(xs[k, 1], w_gu[1], preferred_element_type=F32)
        co["c3"].wait_recv()
        acc[...] += jnp.dot(xs[k, 3], w_gu[3], preferred_element_type=F32)
        co["c2"].wait_recv()
        acc[...] += jnp.dot(xs[k, 2], w_gu[2], preferred_element_type=F32)
        unit = w_gate.shape[1]
        pre = acc[:, :unit]
        hidden = (pre / (1.0 + jnp.exp(-pre)) * acc[:, unit:]).astype(BF16)
        for r in (2, 1, 3, 0):
            parts[k, r] = jnp.dot(hidden, w_dn[r], preferred_element_type=F32).astype(BF16)
            co["p", r] = send(parts.at[k, r, :, THEIRS], crecv.at[k, r], core)

    def chip_sum(k, r, rows):
        return parts[k, r, rows, :feat].astype(F32) + crecv[k, r, rows].astype(F32)

    ALL = pl.ds(0, 2 * half)

    def r1(k):
        co = copies[k]
        co["p", 2].wait_recv()
        ring2[k] = chip_sum(k, 2, ALL).astype(BF16)
        co["g_up"] = send(ring2.at[k, LOW], ring2_in.at[k, LOW], y_up)
        co["g_dn"] = send(ring2.at[k, HIGH], ring2_in.at[k, HIGH], y_dn)
        co["p", 1].wait_recv()
        ring_up[k, half:] = chip_sum(k, 1, HIGH).astype(BF16)
        co["s_up_high"] = send(ring_up.at[k, HIGH], ring_up_in.at[k, HIGH], y_up)
        co["p", 3].wait_recv()
        ring_dn[k, :half] = chip_sum(k, 3, LOW).astype(BF16)
        co["s_dn_low"] = send(ring_dn.at[k, LOW], ring_dn_in.at[k, LOW], y_dn)

    def r2(k):
        co = copies[k]
        co["g_up"].wait_recv()
        ring_up[k, :half] = (chip_sum(k, 1, LOW) + ring2_in[k, :half].astype(F32)).astype(BF16)
        co["s_up_low"] = send(ring_up.at[k, LOW], ring_up_in.at[k, LOW], y_up)
        co["g_dn"].wait_recv()
        ring_dn[k, half:] = (chip_sum(k, 3, HIGH) + ring2_in[k, half:].astype(F32)).astype(BF16)
        co["s_dn_high"] = send(ring_dn.at[k, HIGH], ring_dn_in.at[k, HIGH], y_dn)

    def ring_sum(k, rows):
        return chip_sum(k, 0, rows) + (
            ring_up_in[k, rows].astype(F32) + ring_dn_in[k, rows].astype(F32)
        )

    def r3(k):
        co = copies[k]
        co["p", 0].wait_recv()
        co["s_up_high"].wait_recv()
        co["s_dn_high"].wait_recv()
        xn_out[k] = ring_sum(k, HIGH).astype(BF16)
        co["xn_back"] = send(xn_out.at[k], xn_in.at[k], x_near)
        co["s_up_low"].wait_recv()
        co["s_dn_low"].wait_recv()
        own[k] = ring_sum(k, LOW)

    def r4(k):
        co = copies[k]
        co["xn_back"].wait_recv()
        fin[k] = (own[k] + xn_in[k].astype(F32)).astype(BF16)
        co["xc_back"] = send(fin.at[k, pl.ds(half // 2, half // 2)], xc_in.at[k], x_cross)

    def r5(k):
        copies[k]["xc_back"].wait_recv()
        kept = fin[k, : half // 2].astype(F32)
        crossed = xc_in[k].astype(F32)
        for i, j in enumerate(CHUNKS[k]):
            lo, hi = i * cap, (i + 1) * cap
            block = jnp.concatenate([kept[lo:hi], crossed[lo:hi]], axis=0).astype(BF16)
            if j:
                rets[j] = block
                z_back[j] = send(rets.at[j], retr.at[j], at((z + j) % nz, x, y, c))
            else:
                retr[j] = block

    z_back = {}
    ORDER = (
        (d1, 0), (d2, 0), (d1, 1), (d3, 0), (d2, 1), (d1, 2), (d4, 0), (d3, 1), (d2, 2),
        (d1, 3), (d5, 0), (d3, 2), (d2, 3), (d4, 1), (d3, 3), (compute, 0),
        (r1, 0), (d5, 1), (d4, 2), (compute, 1), (r2, 0), (r1, 1), (d5, 2), (d4, 3),
        (r3, 0), (compute, 2), (r2, 1), (r1, 2), (d5, 3), (r4, 0), (r3, 1), (r5, 0),
        (compute, 3), (r2, 2), (r1, 3), (r4, 1), (r3, 2), (r5, 1), (r2, 3), (r4, 2),
        (r5, 2), (r3, 3), (r4, 3), (r5, 3),
    )
    for stage, k in ORDER:
        stage(k)

    for j in range(1, nz):
        z_back[j].wait_recv()
    back = retr[...].reshape(nz * 2 * cap, feat)
    merged = jnp.dot(slots[...], back, preferred_element_type=F32)
    out[...] = (merged * gate[...].astype(F32)).astype(BF16)
    for copy in started:
        copy.wait_send()


def on_device(nx, ny, nz, tokens, routes, router_gate, w_gate, w_up, w_down):
    rows, feat = tokens.shape
    unit = w_gate.shape[1]
    cap = 3 * rows // (nx * nz)
    half = 4 * cap
    vm = pltpu.VMEM
    scratch = [
        vm((ny, 2 * feat, 2 * unit), BF16),
        vm((ny, unit, 2 * feat), BF16),
        vm((rows, nz * 2 * cap), BF16),
        vm((nz, 2 * cap, feat), BF16),
        vm((nz, 2 * cap, feat), BF16),
        vm((NC, half // 2, feat), BF16),
        vm((NC, ny, 2 * half, 2 * feat), BF16),
        vm((2 * half, 2 * unit), F32),
        vm((NC, ny, 2 * half, 2 * feat), BF16),
        vm((NC, ny, 2 * half, feat), BF16),
    ]
    scratch += [vm((NC, 2 * half, feat), BF16)] * 6
    scratch += [
        vm((NC, half, feat), F32),
        vm((NC, half, feat), BF16),
        vm((NC, half, feat), BF16),
        vm((NC, half, feat), BF16),
        vm((NC, half // 2, feat), BF16),
        vm((nz, 2 * cap, feat), BF16),
        vm((nz, 2 * cap, feat), BF16),
        pltpu.SemaphoreType.DMA((6 * ny,)),
        pltpu.SemaphoreType.DMA((26 * NC + 14,)),
        pltpu.SemaphoreType.DMA((26 * NC + 14,)),
    ]
    in_vmem = pl.BlockSpec(memory_space=pltpu.VMEM)
    in_hbm = pl.BlockSpec(memory_space=pl.ANY)
    return pl.pallas_call(
        functools.partial(kernel, (nx, ny, nz, cap, feat)),
        out_shape=jax.ShapeDtypeStruct((rows, feat), BF16),
        in_specs=[in_vmem] * 3 + [in_hbm] * 3,
        out_specs=in_vmem,
        scratch_shapes=scratch,
        compiler_params=pltpu.CompilerParams(
            collective_id=0, has_side_effects=True, vmem_limit_bytes=60 * 1024 * 1024
        ),
    )(tokens, routes, router_gate, w_gate, w_up, w_down)


def solution(mesh):
    nx, ny = 4, mesh.shape["etp"] // 2
    nz = mesh.shape["ep"] // nx
    return jax.shard_map(
        functools.partial(on_device, nx, ny, nz),
        mesh=mesh,
        in_specs=(
            P("ep", "etp"),
            P("ep", None),
            P("ep", None),
            P(None, ("ep", "etp")),
            P(None, ("ep", "etp")),
            P(("ep", "etp"), None),
        ),
        out_specs=P("ep", "etp"),
        check_vma=False,
    )
```

time: 231 us -> 108 us (0.47)
  waiting for transfers between devices: 126 us -> 0 us
  Pallas kernels: 0 us -> 102 us
  blocking collectives: 37.1 us -> 0 us
  matrix products: 25.4 us -> 0 us
  between operations: 13.5 us -> 0.01 us
  starting transfers between devices: 10.1 us -> 0 us
  local copies, waits for them, and re-layouts: 13.1 us -> 4.62 us
  other arithmetic: 4.37 us -> 0 us
    pallas_call x0 -> x1, Pallas kernels: none -> 102 us  [on_device(): pl.pallas_call(functools.partial(kernel, (nx, ny, nz, cap, feat)), out_sh...]
    unnamed x3 -> x0, waiting for transfers between devices: 52.9 us -> none
    all_gather x1 -> x0, waiting for transfers between devices: 47.8 us -> none  [on_device(): shard_piece = lax.all_gather(received, 'etp', axis=1, tiled=True)]
    all_to_all x1 -> x0, blocking collectives: 37.1 us -> none  [on_device(): lax.all_to_all(doubled, 'ep', split_axis=0, concat_axis=0, tiled=True)]
    all_to_all x1 -> x0, waiting for transfers between devices: 25.7 us -> none  [on_device(): lax.all_to_all(summed.reshape(feat_local, ep_count, capacity).astype(jnp....]
    dot_general x4 -> x0, matrix products: 25.4 us -> none  [the longest x1 16.4 us: on_device(): lax.dot_general(w_down, hidden, (((0,), (1,)), ((), ())), preferred_eleme...]
    all_to_all x1 -> x0, starting transfers between devices: 10.1 us -> none  [on_device(): lax.all_to_all(summed.reshape(feat_local, ep_count, capacity).astype(jnp....]
    unnamed x6 -> x3, local copies, waits for them, and re-layouts: 12.9 us -> 4.62 us
  transfers between devices with their start and end apart: 3 -> 0, of which waited for: 3 -> 0; matrix products, arithmetic and copies ran while one was open for 0% -> 0% of each run, Pallas kernels for 0% -> 0%
where the time goes in v1:
time: 108 us; the launch traced here: 107 us
  Pallas kernels  102 us (94%)
  local copies, waits for them, and re-layouts  4.62 us (4%)
    pallas_call x1, Pallas kernels, on_device(): pl.pallas_call(functools.partial(kernel, (nx, ny, nz, cap, feat)), out_sh...  102 us
    unnamed x3, local copies, waits for them, and re-layouts  4.62 us

profile of v1, /device:TPU:32, one launch (start us, length us, event | category | flops | bytes accessed | tf_op | source)
XLA Modules:
  0.0 106.6 jit_solution(5816350281367519329)
XLA Ops:
  0.0 1.4 %copy.8.gate = bf16[256,1]{1,0:T(8,128)(2,1)} copy(bf16[256,1]{0,1:T(2,128)(2,1)} %param.8) | data formatting | bytes 1024 | tf_op args[2]
  1.4 1.5 %copy.7.routes = s32[256,1]{1,0:T(8,128)} copy(s32[256,1]{0,1:T(1,128)} %param.7) | data formatting | bytes 2048 | tf_op args[1]
  2.9 101.9 %shard_map.64 = bf16[256,640]{1,0:T(8,128)(2,1)} custom-call(bf16[256,640]{1,0:T(8,128)(2,1)} %tokens.1, s32[256,1]{1,0:T(8,128)} %copy.7.routes, bf16[256,1]{1,0:T(8,128)(2,1)} %copy.8.gate, bf16[5120,256]{1,0:T(8,128)(2,1)} %w_gate.1, bf16[5120,256]{1,0:T(8,128)(2,1)} %w_up.1, bf16[256,5120]{1,0:T(8,128)(2,1)} %w_down.1), custom_call_target="tpu_custom_call" | custom-call | tf_op jit(solution)/shard_map/pallas_call | solution.py:289
  104.9 1.7 %copy.10 = bf16[256,640]{1,0:T(8,128)(2,1)} copy(bf16[256,640]{1,0:T(8,128)(2,1)} %shard_map.64) | data formatting | bytes 655360

commit v2 on v1

v2 whole, which is shorter than its diff:
```python
import functools

import jax
import jax.numpy as jnp
from jax import lax
from jax.experimental import pallas as pl
from jax.experimental.pallas import tpu as pltpu
from jax.sharding import PartitionSpec as P

MESH = pl.DeviceIdType.MESH
F32 = jnp.float32
BF16 = jnp.bfloat16

CHUNKS = ((0, 1), (7, 2), (6, 3), (5, 4))
NC = len(CHUNKS)
WIDE_IN = (False, False, False, False)
WIDE_OUT = (False, False, False, False)

ORDER = (
    ("d1", 0), ("d2", 0), ("d1", 1), ("d3", 0), ("d4u", 0), ("d4d", 0), ("d6", 0, 0), ("d2", 1),
    ("d3", 1), ("d1", 2), ("d4a", 0), ("d6", 0, 3), ("d4d", 1), ("d6", 0, 1), ("d1", 3), ("d2", 2),
    ("d6", 1, 0), ("d4u", 1), ("d3", 2), ("d2", 3), ("d4a", 1), ("d5", 0), ("d6", 1, 1), ("d3", 3),
    ("d6", 2, 0), ("d4u", 2), ("d6", 1, 3), ("d4d", 2), ("d6", 3, 0), ("d4u", 3), ("d4a", 2),
    ("d6", 0, 2), ("d5", 1), ("d4d", 3), ("d6", 2, 3), ("c", 0), ("e", 0, 2), ("sC1", 0),
    ("e", 0, 1), ("d4a", 3), ("e", 0, 3), ("gC", 0), ("d5", 2), ("e", 0, 0), ("d6", 1, 2),
    ("d6", 2, 1), ("d6", 3, 3), ("c", 1), ("d5", 3), ("e", 1, 1), ("e", 1, 2), ("sC1", 1),
    ("e", 1, 3), ("sC2", 0), ("e", 1, 0), ("gAB", 0), ("gC", 1), ("d6", 3, 1), ("sAB1", 0),
    ("d6", 2, 2), ("c", 2), ("e", 2, 2), ("sC1", 2), ("e", 2, 1), ("sAB2", 0), ("e", 2, 3),
    ("e", 2, 0), ("sC2", 1), ("gC", 2), ("d6", 3, 2), ("rC", 0), ("sAB1", 1), ("gAB", 1), ("c", 3),
    ("e", 3, 2), ("e", 3, 1), ("sC2", 2), ("sC1", 3), ("e", 3, 3), ("rAB", 0), ("e", 3, 0),
    ("gAB", 2), ("gC", 3), ("sAB2", 1), ("rC", 1), ("rC", 2), ("sAB1", 2), ("r4", 0), ("r5", 0),
    ("sAB2", 2), ("rAB", 1), ("gAB", 3), ("sC2", 3), ("sAB1", 3), ("rAB", 2), ("sAB2", 3),
    ("rC", 3), ("r4", 1), ("r5", 1), ("r4", 2), ("r5", 2), ("rAB", 3), ("r4", 3), ("r5", 3),
)


def kernel(sizes, tokens, routes, gate, w_gate, w_up, w_down, out,
           w_gu, w_dn, slots, outgo, zrecv, cross, xs, acc, parts, crecv, xb_out, xb_in,
           ring2, ring2_in, ring_up, ring_up_in, ring_dn, ring_dn_in,
           own, xn_out, xn_in, fin, fin_x, xc_in, rets, retr,
           w_sem, send_sem, recv_sem):
    nx, ny, nz, cap, feat = sizes
    half, piece = 4 * cap, 2 * cap
    ep = lax.axis_index("ep")
    etp = lax.axis_index("etp")
    z, x = ep // nx, ep % nx
    y, c = etp // 2, etp % 2

    def at(zz, xx, yy, cc):
        return {"ep": zz * nx + xx, "etp": yy * 2 + cc}

    y_up, y_dn = at(z, x, (y + 1) % ny, c), at(z, x, (y + ny - 1) % ny, c)
    core = at(z, x, y, 1 - c)
    x_near = at(z, x + 1 - 2 * (x % 2), y, c)
    x_cross = at(z, nx - 1 - x, y, c)

    barrier = pltpu.get_barrier_semaphore()
    peers = [y_up, y_dn, core, x_near, x_cross] + [
        at((z + j) % nz, x, y, c) for j in range(1, nz)
    ]
    for peer in peers:
        pl.semaphore_signal(barrier, inc=1, device_id=peer, device_id_type=MESH)

    loads = []
    for r in range(ny):
        for k in range(2):
            shard = (((y + r) % ny) * 2 + (c + k) % 2) * feat
            shard = pl.multiple_of(shard, 128)
            into = pl.ds(k * feat, feat)
            unit = w_gate.shape[1]
            loads.append((w_gate.at[pl.ds(shard, feat), :], w_gu.at[r, into, pl.ds(0, unit)]))
            loads.append((w_up.at[pl.ds(shard, feat), :], w_gu.at[r, into, pl.ds(unit, unit)]))
            loads.append((w_down.at[:, pl.ds(shard, feat)], w_dn.at[r, :, into]))
    loads = [pltpu.make_async_copy(a, b, w_sem.at[i]) for i, (a, b) in enumerate(loads)]
    for load in loads:
        load.start()

    rows = routes.shape[1]
    expert = routes[...]
    onehot = (expert == lax.broadcasted_iota(jnp.int32, (nz * nx // 2, rows), 0)).astype(F32)
    before = lax.broadcasted_iota(jnp.int32, (rows, rows), 0) < lax.broadcasted_iota(
        jnp.int32, (rows, rows), 1
    )
    ranks = jnp.dot(onehot.astype(BF16), before.astype(F32).astype(BF16), preferred_element_type=F32)
    rank = jnp.sum(ranks * onehot, axis=0, keepdims=True).astype(jnp.int32)
    unit_of = (z + nz - (expert >> 1)) & (nz - 1)
    other = (expert & 1) != x // 2
    slot = unit_of * (2 * cap) + jnp.where(other, cap, 0) + rank
    place = lax.broadcasted_iota(jnp.int32, (nz * 2 * cap, rows), 0)
    chosen = (slot == place).astype(F32)
    sent = jnp.dot(chosen.astype(BF16), tokens[...], preferred_element_type=F32)
    outgo[...] = sent.astype(BF16).reshape(nz, 2 * cap, feat)
    slots[...] = (chosen * gate[...].astype(F32)).astype(BF16)

    started = []
    used = [0]

    def send(src, dst, device):
        i = used[0]
        used[0] += 1
        copy = pltpu.make_async_remote_copy(
            src_ref=src, dst_ref=dst, send_sem=send_sem.at[i], recv_sem=recv_sem.at[i],
            device_id=device, device_id_type=MESH,
        )
        copy.start()
        started.append(copy)
        return copy

    pl.semaphore_wait(barrier, len(peers))

    z_copy = {}
    for pair in CHUNKS:
        for j in pair:
            if j:
                z_copy[j] = send(outgo.at[j], zrecv.at[j], at((z + nz - j) % nz, x, y, c))

    MINE, THEIRS = pl.ds(0, feat), pl.ds(feat, feat)
    A, B, AB = pl.ds(0, piece), pl.ds(piece, piece), pl.ds(0, half)
    NEAR_A, NEAR_B, NEAR = pl.ds(half, piece), pl.ds(half + piece, piece), pl.ds(half, half)
    copies = [dict() for _ in CHUNKS]

    def wait(k, *names):
        for name in names:
            copy = copies[k][name]
            if copy is not None:
                copy.wait_recv()
                copies[k][name] = None

    def unit_block(j):
        if j:
            z_copy[j].wait_recv()
            return zrecv[j].astype(F32)
        return outgo[j].astype(F32)

    def d1(k):
        co = copies[k]
        first, second = (unit_block(j) for j in CHUNKS[k])
        cross[k] = jnp.concatenate([first[cap:], second[cap:]], axis=0).astype(BF16)
        co["cross"] = send(cross.at[k], xs.at[k, 0, B, MINE], x_cross)
        xs[k, 0, :piece, :feat] = jnp.concatenate([first[:cap], second[:cap]], axis=0).astype(BF16)
        mine = xs.at[k, 0, A, MINE]
        co["xnA"] = send(mine, xs.at[k, 0, NEAR_A, MINE], x_near)
        co["upA"] = send(mine, xs.at[k, 3, A, MINE], y_up)
        co["dnA"] = send(mine, xs.at[k, 1, A, MINE], y_dn)

    def near_b(k, r):
        copies[k]["xnB", r] = send(xs.at[k, r, B, MINE], xs.at[k, r, NEAR_B, MINE], x_near)

    def d2(k):
        co = copies[k]
        wait(k, "cross")
        near_b(k, 0)
        mine = xs.at[k, 0, B, MINE]
        co["upB"] = send(mine, xs.at[k, 3, B, MINE], y_up)
        co["dnB"] = send(mine, xs.at[k, 1, B, MINE], y_dn)
        co["c0"] = send(xs.at[k, 0, AB, MINE], xs.at[k, 0, AB, THEIRS], core)

    def d3(k):
        co = copies[k]
        wait(k, "xnA")
        if WIDE_IN[k]:
            wait(k, ("xnB", 0))
        rows_c = NEAR if WIDE_IN[k] else NEAR_A
        mine = xs.at[k, 0, rows_c, MINE]
        co["upC"] = send(mine, xs.at[k, 3, rows_c, MINE], y_up)
        co["dnC"] = send(mine, xs.at[k, 1, rows_c, MINE], y_dn)
        co["c0C"] = send(mine, xs.at[k, 0, rows_c, THEIRS], core)

    def pass_on(k, r, rows_of):
        src, device = ((3, y_up) if r > 0 else (1, y_dn))
        return send(xs.at[k, src, rows_of, MINE], xs.at[k, 2, rows_of, MINE], device)

    def d4u(k):
        wait(k, "upA", "upB")
        if not WIDE_IN[k]:
            near_b(k, 3)
        if k % 2 == 0:
            copies[k]["fAB"] = pass_on(k, 1, AB)

    def d4d(k):
        wait(k, "dnA", "dnB")
        if not WIDE_IN[k]:
            near_b(k, 1)
        if k % 2:
            copies[k]["fAB"] = pass_on(k, -1, AB)

    def to_core(k, r):
        rows_of = pl.ds(0, 2 * half if WIDE_IN[k] else half + piece)
        copies[k]["c", r] = send(xs.at[k, r, rows_of, MINE], xs.at[k, r, rows_of, THEIRS], core)

    def d4a(k):
        wait(k, "upA", "upB", "dnA", "dnB", "upC", "dnC")
        copies[k]["fC"] = pass_on(k, 1 if k % 2 else -1, NEAR if WIDE_IN[k] else NEAR_A)
        to_core(k, 1)
        to_core(k, 3)

    def d5(k):
        wait(k, "fAB", "fC")
        if not WIDE_IN[k]:
            near_b(k, 2)
        to_core(k, 2)

    def d6(k, r):
        if not WIDE_IN[k]:
            wait(k, ("xnB", r))
            copies[k]["cB", r] = send(xs.at[k, r, NEAR_B, MINE], xs.at[k, r, NEAR_B, THEIRS], core)

    def compute(k):
        co = copies[k]
        if k == 0:
            for load in loads:
                load.wait()
        for i, r in enumerate((0, 1, 3, 2)):
            wait(k, *(("c0", "c0C") if r == 0 else (("c", r),)))
            if not WIDE_IN[k]:
                wait(k, ("cB", r))
            pre = jnp.dot(xs[k, r], w_gu[r], preferred_element_type=F32)
            acc[...] = pre if i == 0 else acc[...] + pre
        unit = w_gate.shape[1]
        pre = acc[:, :unit]
        hidden = (pre / (1.0 + jnp.exp(-pre)) * acc[:, unit:]).astype(BF16)
        for r in (2, 1, 3, 0):
            parts[k, r] = jnp.dot(hidden, w_dn[r], preferred_element_type=F32).astype(BF16)
            co["p", r] = send(parts.at[k, r, :, THEIRS], crecv.at[k, r], core)

    def chip_sum(k, r, rows_of):
        return parts[k, r, rows_of, :feat].astype(F32) + crecv[k, r, rows_of].astype(F32)

    def b_sum(k, r):
        if WIDE_OUT[k]:
            return chip_sum(k, r, B)
        return chip_sum(k, r, B) + xb_in[k, r].astype(F32)

    def c_rows(k):
        return NEAR if WIDE_OUT[k] else NEAR_A

    def e(k, r):
        wait(k, ("p", r))
        if not WIDE_OUT[k]:
            xb_out[k, r] = chip_sum(k, r, NEAR_B).astype(BF16)
            copies[k]["xb", r] = send(xb_out.at[k, r], xb_in.at[k, r], x_near)

    def wait_b(k, r):
        wait(k, ("p", r))
        if not WIDE_OUT[k]:
            wait(k, ("xb", r))

    def gC(k):
        wait(k, ("p", 2))
        ring2[k, c_rows(k)] = chip_sum(k, 2, c_rows(k)).astype(BF16)
        copies[k]["gC"] = send(
            ring2.at[k, c_rows(k)], ring2_in.at[k, c_rows(k)], y_up if k % 2 else y_dn
        )

    def gAB(k):
        wait_b(k, 2)
        ring2[k, A] = chip_sum(k, 2, A).astype(BF16)
        ring2[k, B] = b_sum(k, 2).astype(BF16)
        copies[k]["gAB"] = send(ring2.at[k, AB], ring2_in.at[k, AB], y_dn if k % 2 else y_up)

    def way(k, up):
        return (1, ring_up, ring_up_in, y_up) if up else (3, ring_dn, ring_dn_in, y_dn)

    def sC1(k):
        r, buf, into, device = way(k, k % 2 == 0)
        wait(k, ("p", r))
        buf[k, c_rows(k)] = chip_sum(k, r, c_rows(k)).astype(BF16)
        copies[k]["s1C"] = send(buf.at[k, c_rows(k)], into.at[k, c_rows(k)], device)

    def sAB1(k):
        r, buf, into, device = way(k, k % 2 == 1)
        wait_b(k, r)
        buf[k, A] = chip_sum(k, r, A).astype(BF16)
        buf[k, B] = b_sum(k, r).astype(BF16)
        copies[k]["s1AB"] = send(buf.at[k, AB], into.at[k, AB], device)

    def sAB2(k):
        r, buf, into, device = way(k, k % 2 == 0)
        wait_b(k, r)
        wait(k, "gAB")
        buf[k, A] = (chip_sum(k, r, A) + ring2_in[k, A].astype(F32)).astype(BF16)
        buf[k, B] = (b_sum(k, r) + ring2_in[k, B].astype(F32)).astype(BF16)
        copies[k]["s2AB"] = send(buf.at[k, AB], into.at[k, AB], device)

    def sC2(k):
        r, buf, into, device = way(k, k % 2 == 1)
        wait(k, ("p", r), "gC")
        rows_of = c_rows(k)
        buf[k, rows_of] = (chip_sum(k, r, rows_of) + ring2_in[k, rows_of].astype(F32)).astype(BF16)
        copies[k]["s2C"] = send(buf.at[k, rows_of], into.at[k, rows_of], device)

    def neighbours(k, rows_of):
        return ring_up_in[k, rows_of].astype(F32) + ring_dn_in[k, rows_of].astype(F32)

    def rC(k):
        wait(k, ("p", 0), "s1C", "s2C")
        rows_of = c_rows(k)
        into = AB if WIDE_OUT[k] else A
        xn_out[k, into] = (chip_sum(k, 0, rows_of) + neighbours(k, rows_of)).astype(BF16)
        copies[k]["xnback"] = send(xn_out.at[k, into], xn_in.at[k, into], x_near)

    def rAB(k):
        wait_b(k, 0)
        wait(k, "s1AB", "s2AB")
        crossing = b_sum(k, 0) + neighbours(k, B)
        if WIDE_OUT[k]:
            wait(k, "xnback")
            crossing = crossing + xn_in[k, B].astype(F32)
        fin_x[k] = crossing.astype(BF16)
        copies[k]["xcback"] = send(fin_x.at[k], xc_in.at[k], x_cross)
        own[k] = chip_sum(k, 0, A) + neighbours(k, A)

    def r4(k):
        wait(k, "xnback")
        fin[k] = own[k] + xn_in[k, A].astype(F32)

    def r5(k):
        wait(k, "xcback")
        kept = fin[k]
        crossed = xc_in[k].astype(F32)
        for i, j in enumerate(CHUNKS[k]):
            lo, hi = i * cap, (i + 1) * cap
            block = jnp.concatenate([kept[lo:hi], crossed[lo:hi]], axis=0).astype(BF16)
            if j:
                rets[j] = block
                z_back[j] = send(rets.at[j], retr.at[j], at((z + j) % nz, x, y, c))
            else:
                retr[j] = block

    z_back = {}
    STAGES = dict(
        d1=d1, d2=d2, d3=d3, d4u=d4u, d4d=d4d, d4a=d4a, d5=d5, d6=d6, c=compute, e=e, gC=gC, gAB=gAB,
        sC1=sC1, sAB1=sAB1, sAB2=sAB2, sC2=sC2, rC=rC, rAB=rAB, r4=r4, r5=r5,
    )
    for name, *where in ORDER:
        STAGES[name](*where)

    for j in range(1, nz):
        z_back[j].wait_recv()
    back = retr[...].reshape(nz * 2 * cap, feat)
    merged = lax.dot_general(
        slots[...], back, (((0,), (0,)), ((), ())), preferred_element_type=F32
    )
    out[...] = merged.astype(BF16)
    for copy in started:
        copy.wait_send()


def on_device(nx, ny, nz, tokens, routes, router_gate, w_gate, w_up, w_down):
    rows, feat = tokens.shape
    unit = w_gate.shape[1]
    cap = 3 * rows // (nx * nz)
    half, piece = 4 * cap, 2 * cap
    vm = pltpu.VMEM
    scratch = [
        vm((ny, 2 * feat, 2 * unit), BF16),
        vm((ny, unit, 2 * feat), BF16),
        vm((nz * 2 * cap, rows), BF16),
        vm((nz, 2 * cap, feat), BF16),
        vm((nz, 2 * cap, feat), BF16),
        vm((NC, piece, feat), BF16),
        vm((NC, ny, 2 * half, 2 * feat), BF16),
        vm((2 * half, 2 * unit), F32),
        vm((NC, ny, 2 * half, 2 * feat), BF16),
        vm((NC, ny, 2 * half, feat), BF16),
        vm((NC, ny, piece, feat), BF16),
        vm((NC, ny, piece, feat), BF16),
    ]
    scratch += [vm((NC, 2 * half, feat), BF16)] * 6
    scratch += [
        vm((NC, piece, feat), F32),
        vm((NC, half, feat), BF16),
        vm((NC, half, feat), BF16),
        vm((NC, piece, feat), F32),
        vm((NC, piece, feat), BF16),
        vm((NC, piece, feat), BF16),
        vm((nz, 2 * cap, feat), BF16),
        vm((nz, 2 * cap, feat), BF16),
        pltpu.SemaphoreType.DMA((6 * ny,)),
        pltpu.SemaphoreType.DMA((44 * NC + 14,)),
        pltpu.SemaphoreType.DMA((44 * NC + 14,)),
    ]
    in_vmem = pl.BlockSpec(memory_space=pltpu.VMEM)
    in_hbm = pl.BlockSpec(memory_space=pl.ANY)
    return pl.pallas_call(
        functools.partial(kernel, (nx, ny, nz, cap, feat)),
        out_shape=jax.ShapeDtypeStruct((rows, feat), BF16),
        in_specs=[in_vmem] * 3 + [in_hbm] * 3,
        out_specs=in_vmem,
        scratch_shapes=scratch,
        compiler_params=pltpu.CompilerParams(
            collective_id=0, has_side_effects=True, vmem_limit_bytes=60 * 1024 * 1024
        ),
    )(tokens, routes.reshape(1, rows), router_gate.reshape(1, rows), w_gate, w_up, w_down)


def solution(mesh):
    nx, ny = 4, mesh.shape["etp"] // 2
    nz = mesh.shape["ep"] // nx
    return jax.shard_map(
        functools.partial(on_device, nx, ny, nz),
        mesh=mesh,
        in_specs=(
            P("ep", "etp"),
            P("ep", None),
            P("ep", None),
            P(None, ("ep", "etp")),
            P(None, ("ep", "etp")),
            P(("ep", "etp"), None),
        ),
        out_specs=P("ep", "etp"),
        check_vma=False,
    )
```

time: 108 us -> 92.7 us (0.86); the launches traced: 107 us -> 92.6 us
  Pallas kernels: 102 us -> 90.9 us
  local copies, waits for them, and re-layouts: 4.62 us -> 1.73 us
    pallas_call x1, Pallas kernels: 102 us -> 90.9 us  [on_device(): pl.pallas_call(functools.partial(kernel, (nx, ny, nz, cap, feat)), out_sh...]
    unnamed x3 -> x1, local copies, waits for them, and re-layouts: 4.62 us -> 1.73 us
where the time goes in v2:
time: 92.7 us; the launch traced here: 92.6 us
  Pallas kernels  90.9 us (98%)
  local copies, waits for them, and re-layouts  1.73 us (2%)
    pallas_call x1, Pallas kernels, on_device(): pl.pallas_call(functools.partial(kernel, (nx, ny, nz, cap, feat)), out_sh...  90.9 us

profile of v2, /device:TPU:32, one launch (start us, length us, event | category | flops | bytes accessed | tf_op | source)
XLA Modules:
  0.0 92.6 jit_solution(14490477065963556940)
XLA Ops:
  0.0 90.9 %shard_map.64 = bf16[256,640]{1,0:T(8,128)(2,1)} custom-call(bf16[256,640]{1,0:T(8,128)(2,1)} %tokens.1, s32[1,256]{1,0:T(1,128)} %bitcast.2, bf16[1,256]{1,0:T(2,128)(2,1)} %bitcast.3, bf16[5120,256]{1,0:T(8,128)(2,1)} %w_gate.1, bf16[5120,256]{1,0:T(8,128)(2,1)} %w_up.1, bf16[256,5120]{1,0:T(8,128)(2,1)} %w_down.1), custom_call_target="tpu_custom_call" | custom-call | tf_op jit(solution)/shard_map/pallas_call | solution.py:385
  90.9 1.7 %copy.8 = bf16[256,640]{1,0:T(8,128)(2,1)} copy(bf16[256,640]{1,0:T(8,128)(2,1)} %shard_map.64) | data formatting | bytes 655360

commit v3 on v2

v3 whole, which is shorter than its diff:
```python
import functools

import jax
import jax.numpy as jnp
from jax import lax
from jax.experimental import pallas as pl
from jax.experimental.pallas import tpu as pltpu
from jax.sharding import PartitionSpec as P

MESH = pl.DeviceIdType.MESH
F32 = jnp.float32
BF16 = jnp.bfloat16

PAIRS = ((0, 1), (6, 3), (5, 4), (7, 2))
CHUNKS = (
    (0, 0, 16),
    (0, 16, 48),
    (1, 0, 48),
    (2, 0, 48),
    (3, 0, 32),
    (3, 32, 48),
)
WIDE_IN = (0, 0, 0, 0, 0, 0)
WIDE_OUT = (0, 0, 0, 0, 0, 0)
STRAIGHT_IN = (0, 0, 0, 0, 0, 0)
STRAIGHT_OUT = (0, 0, 0, 0, 0, 0)
FLIP = (0, 1, 0, 1, 0, 1)
NC = len(CHUNKS)
SEMS = (49, 102)
Z_ORDER = (1, 7, 6, 2, 3, 5, 4)


ORDER = (
    ("d1", 0), ("d2", 0), ("d3", 0), ("d1", 1), ("d6", 0, 0), ("d4d", 0), ("d4u", 0), ("d4a", 0),
    ("d2", 1), ("d1", 5), ("d1", 4), ("d3", 1), ("d5", 0), ("d2", 5), ("d4u", 1), ("d3", 5),
    ("d2", 4), ("d3", 4), ("d1", 2), ("d4d", 5), ("d6", 0, 1), ("d4a", 1), ("d4a", 5), ("d6", 0, 3),
    ("d6", 5, 0), ("d4d", 1), ("d6", 0, 2), ("d4u", 4), ("d2", 2), ("d1", 3), ("c", 0),
    ("d6", 1, 0), ("d5", 5), ("d4u", 5), ("d5", 1), ("d6", 1, 1), ("d6", 1, 3), ("d6", 4, 0),
    ("d4a", 4), ("d6", 5, 1), ("d4d", 4), ("d3", 2), ("d6", 4, 3), ("d6", 2, 0), ("d2", 3),
    ("d6", 5, 3), ("d6", 5, 2), ("d3", 3), ("d4d", 2), ("d4u", 2), ("d6", 1, 2), ("d5", 4),
    ("c", 5), ("d4a", 2), ("e", 5, 1), ("d4d", 3), ("c", 1), ("d4a", 3), ("d4u", 3), ("d6", 4, 2),
    ("gC", 5), ("d6", 4, 1), ("sC1", 5), ("gC", 0), ("d5", 2), ("e", 1, 2), ("c", 4), ("d5", 3),
    ("e", 5, 2), ("d6", 3, 0), ("sC1", 0), ("gC", 1), ("e", 5, 0), ("d6", 2, 3), ("d6", 2, 1),
    ("d6", 3, 3), ("gC", 4), ("e", 4, 2), ("d6", 2, 2), ("sC1", 4), ("e", 4, 3), ("e", 1, 3),
    ("sC2", 5), ("e", 5, 3), ("gAB", 1), ("c", 2), ("d6", 3, 2), ("gAB", 5), ("sAB1", 5),
    ("e", 2, 2), ("e", 0, 2), ("e", 4, 1), ("e", 2, 1), ("d6", 3, 1), ("sC1", 2), ("gC", 2),
    ("gAB", 4), ("e", 0, 3), ("sAB1", 4), ("c", 3), ("gAB", 2), ("sC2", 4), ("sAB2", 5),
    ("e", 3, 2), ("e", 4, 0), ("e", 2, 3), ("rC", 5), ("gC", 3), ("sC1", 3), ("e", 3, 1),
    ("e", 3, 3), ("sC2", 2), ("gAB", 0), ("e", 2, 0), ("sAB2", 4), ("gAB", 3), ("sAB2", 2),
    ("rAB", 5), ("e", 1, 1), ("sAB1", 2), ("rC", 4), ("sC2", 3), ("r4", 5), ("rAB", 4), ("sAB2", 3),
    ("e", 3, 0), ("sAB1", 3), ("sC2", 0), ("sC1", 1), ("rC", 2), ("sAB1", 1), ("sC2", 1),
    ("rAB", 2), ("r4", 4), ("e", 0, 0), ("r5", 4), ("sAB2", 1), ("r5", 5), ("e", 0, 1), ("e", 1, 0),
    ("rC", 3), ("rC", 0), ("rAB", 3), ("r4", 2), ("r5", 2), ("sAB2", 0), ("sAB1", 0), ("r4", 3),
    ("rAB", 1), ("rC", 1), ("r5", 3), ("rAB", 0), ("r4", 1), ("r4", 0), ("r5", 0), ("r5", 1),
)

BACK = {"up": "dn", "dn": "up", "two": "two", "core": "core", "near": "near", "cross": "cross"}


def kernel(sizes, tokens, routes, gate, w_gate, w_up, w_down, out,
           w_gu, w_dn, outgo, zrecv, cross, xs, acc, parts, crecv, xb_out, xb_in,
           ring2, ring2_in, ring_up, ring_up_in, ring_dn, ring_dn_in,
           own, xn_out, xn_in, fin, fin_x, xc_in, rets, retr, tok, slots_t,
           t_sem, w_sem, send_sem, recv_sem):
    nx, ny, nz, cap, feat = sizes
    ep = lax.axis_index("ep")
    etp = lax.axis_index("etp")
    z, x = ep // nx, ep % nx
    y, c = etp // 2, etp % 2

    def at(zz, xx, yy, cc):
        return {"ep": zz * nx + xx, "etp": yy * 2 + cc}

    y_up, y_dn = ("up", at(z, x, (y + 1) % ny, c)), ("dn", at(z, x, (y + ny - 1) % ny, c))
    y_two = ("two", at(z, x, (y + 2) % ny, c))
    core = ("core", at(z, x, y, 1 - c))
    x_near = ("near", at(z, x + 1 - 2 * (x % 2), y, c))
    x_cross = ("cross", at(z, nx - 1 - x, y, c))

    load_tokens = pltpu.make_async_copy(tokens, tok, t_sem)
    load_tokens.start()
    barrier = pltpu.get_barrier_semaphore()
    peers = [to[1] for to in (y_up, y_dn, core, x_near, x_cross)]
    if any(STRAIGHT_IN + STRAIGHT_OUT):
        peers.append(y_two[1])
    peers += [at((z + j) % nz, x, y, c) for j in range(1, nz)]
    for peer in peers:
        pl.semaphore_signal(barrier, inc=1, device_id=peer, device_id_type=MESH)

    rows = routes.shape[1]
    expert = routes[...]
    onehot = (expert == lax.broadcasted_iota(jnp.int32, (nz * nx // 2, rows), 0)).astype(F32)
    before = lax.broadcasted_iota(jnp.int32, (rows, rows), 0) < lax.broadcasted_iota(
        jnp.int32, (rows, rows), 1
    )
    ranks = jnp.dot(onehot.astype(BF16), before.astype(F32).astype(BF16), preferred_element_type=F32)
    rank = jnp.sum(ranks * onehot, axis=0, keepdims=True).astype(jnp.int32)
    unit_of = (z + nz - (expert >> 1)) & (nz - 1)
    other = (expert & 1) != x // 2
    slot = unit_of * (2 * cap) + jnp.where(other, cap, 0) + rank
    place = lax.broadcasted_iota(jnp.int32, (nz * 2 * cap, rows), 0)
    chosen = (slot == place).astype(F32)
    load_tokens.wait()
    sent = jnp.dot(chosen.astype(BF16), tok[...], preferred_element_type=F32)
    outgo[...] = sent.astype(BF16).reshape(nz, 2 * cap, feat)
    clock, used = [0], [0, 0]
    heard = dict.fromkeys(BACK, -1)
    free_send, free_recv = [], []

    def send(src, dst, to):
        link, device = to
        clock[0] += 1
        if free_send:
            i = free_send.pop()
        else:
            i = used[0]
            used[0] += 1
        ready = [at_ for at_ in free_recv if link in BACK and at_[0] < heard[BACK[link]]]
        if ready:
            free_recv.remove(ready[0])
            j = ready[0][1]
        else:
            j = used[1]
            used[1] += 1
        copy = pltpu.make_async_remote_copy(
            src_ref=src, dst_ref=dst, send_sem=send_sem.at[i], recv_sem=recv_sem.at[j],
            device_id=device, device_id_type=MESH,
        )
        copy.start()
        return copy, link, clock[0], i, j

    def finish(flight):
        copy, link, sent_at, i, j = flight
        copy.wait_recv()
        copy.wait_send()
        clock[0] += 1
        if link in BACK:
            heard[link] = max(heard[link], sent_at)
        free_send.append(i)
        free_recv.append((clock[0], j))

    pl.semaphore_wait(barrier, len(peers))

    z_copy = {}
    for j in Z_ORDER:
        z_copy[j] = send(outgo.at[j], zrecv.at[j], ("z", at((z + nz - j) % nz, x, y, c)))

    unit = w_gate.shape[1]
    for r in range(ny):
        for k in range(2):
            shard = pl.ds(pl.multiple_of((((y + r) % ny) * 2 + (c + k) % 2) * feat, 128), feat)
            into = pl.ds(k * feat, feat)
            for source, target, sem in (
                (w_gate.at[shard, :], w_gu.at[r, into, pl.ds(0, unit)], 0),
                (w_up.at[shard, :], w_gu.at[r, into, pl.ds(unit, unit)], 0),
                (w_down.at[:, shard], w_dn.at[r, :, into], 1),
            ):
                pltpu.make_async_copy(source, target, w_sem.at[sem]).start()
    loads = [pltpu.make_async_copy(w, w, w_sem.at[i]) for i, w in enumerate((w_gu, w_dn))]

    slots_t[...] = (chosen * gate[...].astype(F32)).T.astype(BF16)

    MINE, THEIRS = pl.ds(0, feat), pl.ds(feat, feat)
    n_of = [hi - lo for _, lo, hi in CHUNKS]

    def A(k):
        return pl.ds(0, n_of[k])

    def B(k):
        return pl.ds(n_of[k], n_of[k])

    def AB(k):
        return pl.ds(0, 2 * n_of[k])

    def NEAR_A(k):
        return pl.ds(2 * n_of[k], n_of[k])

    def NEAR_B(k):
        return pl.ds(3 * n_of[k], n_of[k])

    def C_IN(k):
        return pl.ds(2 * n_of[k], (2 if WIDE_IN[k] else 1) * n_of[k])

    def C_OUT(k):
        return pl.ds(2 * n_of[k], (2 if WIDE_OUT[k] else 1) * n_of[k])

    copies = [dict() for _ in CHUNKS]

    def wait(k, *names):
        for name in names:
            flight = copies[k][name]
            if flight is not None:
                finish(flight)
                copies[k][name] = None

    def take(k, off):
        pair, lo, hi = CHUNKS[k]
        found = []
        for i, j in enumerate(PAIRS[pair]):
            first, last = max(lo - i * cap, 0), min(hi - i * cap, cap)
            if first < last:
                if j in z_copy:
                    finish(z_copy.pop(j))
                block = (zrecv if j else outgo)[j].astype(F32)
                found.append(block[off + first : off + last])
        return jnp.concatenate(found, axis=0).astype(BF16) if len(found) > 1 else found[0].astype(BF16)

    def d1(k):
        co = copies[k]
        cross[k, A(k)] = take(k, cap)
        co["cross"] = send(cross.at[k, A(k)], xs.at[k, 0, B(k), MINE], x_cross)
        xs[k, 0, A(k), :feat] = take(k, 0)
        mine = xs.at[k, 0, A(k), MINE]
        co["xnA"] = send(mine, xs.at[k, 0, NEAR_A(k), MINE], x_near)
        co["upA"] = send(mine, xs.at[k, 3, A(k), MINE], y_up)
        co["dnA"] = send(mine, xs.at[k, 1, A(k), MINE], y_dn)
        if STRAIGHT_IN[k]:
            co["y2A"] = send(mine, xs.at[k, 2, A(k), MINE], y_two)

    def near_b(k, r):
        copies[k]["xnB", r] = send(xs.at[k, r, B(k), MINE], xs.at[k, r, NEAR_B(k), MINE], x_near)

    def d2(k):
        co = copies[k]
        wait(k, "cross")
        near_b(k, 0)
        mine = xs.at[k, 0, B(k), MINE]
        co["upB"] = send(mine, xs.at[k, 3, B(k), MINE], y_up)
        co["dnB"] = send(mine, xs.at[k, 1, B(k), MINE], y_dn)
        if STRAIGHT_IN[k]:
            co["y2B"] = send(mine, xs.at[k, 2, B(k), MINE], y_two)
        co["c0"] = send(xs.at[k, 0, AB(k), MINE], xs.at[k, 0, AB(k), THEIRS], core)

    def d3(k):
        co = copies[k]
        wait(k, "xnA")
        if WIDE_IN[k]:
            wait(k, ("xnB", 0))
        rows_c = C_IN(k)
        mine = xs.at[k, 0, rows_c, MINE]
        co["upC"] = send(mine, xs.at[k, 3, rows_c, MINE], y_up)
        co["dnC"] = send(mine, xs.at[k, 1, rows_c, MINE], y_dn)
        if STRAIGHT_IN[k]:
            co["y2C"] = send(mine, xs.at[k, 2, rows_c, MINE], y_two)
        co["c0C"] = send(mine, xs.at[k, 0, rows_c, THEIRS], core)

    def pass_on(k, up, rows_of):
        src, device = (3, y_up) if up else (1, y_dn)
        return send(xs.at[k, src, rows_of, MINE], xs.at[k, 2, rows_of, MINE], device)

    def up_AB(k):
        return not FLIP[k]

    def d4u(k):
        wait(k, "upA", "upB")
        if not WIDE_IN[k]:
            near_b(k, 3)
        if up_AB(k) and not STRAIGHT_IN[k]:
            copies[k]["fAB"] = pass_on(k, True, AB(k))

    def d4d(k):
        wait(k, "dnA", "dnB")
        if not WIDE_IN[k]:
            near_b(k, 1)
        if not up_AB(k) and not STRAIGHT_IN[k]:
            copies[k]["fAB"] = pass_on(k, False, AB(k))

    def to_core(k, r):
        rows_of = pl.ds(0, (4 if WIDE_IN[k] else 3) * n_of[k])
        copies[k]["c", r] = send(xs.at[k, r, rows_of, MINE], xs.at[k, r, rows_of, THEIRS], core)

    def d4a(k):
        wait(k, "upA", "upB", "dnA", "dnB", "upC", "dnC")
        if not STRAIGHT_IN[k]:
            copies[k]["fC"] = pass_on(k, not up_AB(k), C_IN(k))
        to_core(k, 1)
        to_core(k, 3)

    def d5(k):
        wait(k, *(("y2A", "y2B", "y2C") if STRAIGHT_IN[k] else ("fAB", "fC")))
        if not WIDE_IN[k]:
            near_b(k, 2)
        to_core(k, 2)

    def d6(k, r):
        if not WIDE_IN[k]:
            wait(k, ("xnB", r))
            mine = xs.at[k, r, NEAR_B(k), MINE]
            copies[k]["cB", r] = send(mine, xs.at[k, r, NEAR_B(k), THEIRS], core)

    def compute(k):
        co = copies[k]
        while loads:
            loads.pop().wait()
        whole = pl.ds(0, 4 * n_of[k])
        for i, r in enumerate((0, 1, 3, 2)):
            wait(k, *(("c0", "c0C") if r == 0 else (("c", r),)))
            if not WIDE_IN[k]:
                wait(k, ("cB", r))
            pre = jnp.dot(xs[k, r, whole, :], w_gu[r], preferred_element_type=F32)
            acc[whole, :] = pre if i == 0 else acc[whole, :] + pre
        unit = w_gate.shape[1]
        pre = acc[whole, :unit]
        hidden = (pre / (1.0 + jnp.exp(-pre)) * acc[whole, unit:]).astype(BF16)
        for r in (2, 1, 3, 0):
            parts[k, r, whole, :] = jnp.dot(
                hidden, w_dn[r], preferred_element_type=F32
            ).astype(BF16)
            co["p", r] = send(parts.at[k, r, whole, THEIRS], crecv.at[k, r, whole], core)

    def chip_sum(k, r, rows_of):
        return parts[k, r, rows_of, :feat].astype(F32) + crecv[k, r, rows_of].astype(F32)

    def b_sum(k, r):
        if WIDE_OUT[k]:
            return chip_sum(k, r, B(k))
        return chip_sum(k, r, B(k)) + xb_in[k, r, A(k)].astype(F32)

    def e(k, r):
        wait(k, ("p", r))
        if not WIDE_OUT[k]:
            xb_out[k, r, A(k)] = chip_sum(k, r, NEAR_B(k)).astype(BF16)
            copies[k]["xb", r] = send(xb_out.at[k, r, A(k)], xb_in.at[k, r, A(k)], x_near)

    def wait_b(k, r):
        wait(k, ("p", r))
        if not WIDE_OUT[k]:
            wait(k, ("xb", r))

    def gC(k):
        wait(k, ("p", 2))
        rows_of = C_OUT(k)
        ring2[k, rows_of] = chip_sum(k, 2, rows_of).astype(BF16)
        device = y_two if STRAIGHT_OUT[k] else y_dn if up_AB(k) else y_up
        copies[k]["gC"] = send(ring2.at[k, rows_of], ring2_in.at[k, rows_of], device)

    def gAB(k):
        wait_b(k, 2)
        ring2[k, A(k)] = chip_sum(k, 2, A(k)).astype(BF16)
        ring2[k, B(k)] = b_sum(k, 2).astype(BF16)
        device = y_two if STRAIGHT_OUT[k] else y_up if up_AB(k) else y_dn
        copies[k]["gAB"] = send(ring2.at[k, AB(k)], ring2_in.at[k, AB(k)], device)

    def way(k, up):
        return (1, ring_up, ring_up_in, y_up) if up else (3, ring_dn, ring_dn_in, y_dn)

    def passing(k, name, rows_of):
        if STRAIGHT_OUT[k]:
            return 0.0
        wait(k, name)
        return ring2_in[k, rows_of].astype(F32)

    def sC1(k):
        r, buf, into, device = way(k, up_AB(k))
        wait(k, ("p", r))
        rows_of = C_OUT(k)
        buf[k, rows_of] = chip_sum(k, r, rows_of).astype(BF16)
        copies[k]["s1C"] = send(buf.at[k, rows_of], into.at[k, rows_of], device)

    def sAB1(k):
        r, buf, into, device = way(k, not up_AB(k))
        wait_b(k, r)
        buf[k, A(k)] = chip_sum(k, r, A(k)).astype(BF16)
        buf[k, B(k)] = b_sum(k, r).astype(BF16)
        copies[k]["s1AB"] = send(buf.at[k, AB(k)], into.at[k, AB(k)], device)

    def sAB2(k):
        r, buf, into, device = way(k, up_AB(k))
        wait_b(k, r)
        buf[k, A(k)] = (chip_sum(k, r, A(k)) + passing(k, "gAB", A(k))).astype(BF16)
        buf[k, B(k)] = (b_sum(k, r) + passing(k, "gAB", B(k))).astype(BF16)
        copies[k]["s2AB"] = send(buf.at[k, AB(k)], into.at[k, AB(k)], device)

    def sC2(k):
        r, buf, into, device = way(k, not up_AB(k))
        wait(k, ("p", r))
        rows_of = C_OUT(k)
        buf[k, rows_of] = (chip_sum(k, r, rows_of) + passing(k, "gC", rows_of)).astype(BF16)
        copies[k]["s2C"] = send(buf.at[k, rows_of], into.at[k, rows_of], device)

    def neighbours(k, rows_of):
        both = ring_up_in[k, rows_of].astype(F32) + ring_dn_in[k, rows_of].astype(F32)
        if STRAIGHT_OUT[k]:
            both = both + ring2_in[k, rows_of].astype(F32)
        return both

    def rC(k):
        wait(k, ("p", 0), "s1C", "s2C")
        if STRAIGHT_OUT[k]:
            wait(k, "gC")
        rows_of = C_OUT(k)
        into = AB(k) if WIDE_OUT[k] else A(k)
        xn_out[k, into] = (chip_sum(k, 0, rows_of) + neighbours(k, rows_of)).astype(BF16)
        copies[k]["xnback"] = send(xn_out.at[k, into], xn_in.at[k, into], x_near)

    def rAB(k):
        pair, lo, hi = CHUNKS[k]
        wait_b(k, 0)
        wait(k, "s1AB", "s2AB")
        if STRAIGHT_OUT[k]:
            wait(k, "gAB")
        crossing = b_sum(k, 0) + neighbours(k, B(k))
        if WIDE_OUT[k]:
            wait(k, "xnback")
            crossing = crossing + xn_in[k, B(k)].astype(F32)
        fin_x[k, A(k)] = crossing.astype(BF16)
        copies[k]["xcback"] = send(
            fin_x.at[k, A(k)], xc_in.at[pair, pl.ds(lo, hi - lo)], x_cross
        )
        own[k, A(k)] = chip_sum(k, 0, A(k)) + neighbours(k, A(k))

    def r4(k):
        pair, lo, hi = CHUNKS[k]
        wait(k, "xnback")
        fin[pair, lo:hi] = own[k, A(k)] + xn_in[k, A(k)].astype(F32)

    def r5(k):
        wait(k, "xcback")
        pair, lo, hi = CHUNKS[k]
        for i, j in enumerate(PAIRS[pair]):
            first, last = i * cap, (i + 1) * cap
            if lo < last <= hi:
                kept, crossed = fin[pair, first:last], xc_in[pair, first:last].astype(F32)
                block = jnp.concatenate([kept, crossed], axis=0).astype(BF16)
                if j:
                    rets[j] = block
                    z_back[j] = send(rets.at[j], retr.at[j], ("z", at((z + j) % nz, x, y, c)))
                else:
                    retr[j] = block

    z_back = {}
    STAGES = dict(
        d1=d1, d2=d2, d3=d3, d4u=d4u, d4d=d4d, d4a=d4a, d5=d5, d6=d6, c=compute, e=e, gC=gC, gAB=gAB,
        sC1=sC1, sAB1=sAB1, sAB2=sAB2, sC2=sC2, rC=rC, rAB=rAB, r4=r4, r5=r5,
    )
    for name, *where in ORDER:
        STAGES[name](*where)

    for j in range(1, nz):
        finish(z_back[j])
    back = retr[...].reshape(nz * 2 * cap, feat)
    merged = jnp.dot(slots_t[...], back, preferred_element_type=F32)
    out[...] = merged.astype(BF16)


def on_device(nx, ny, nz, tokens, routes, router_gate, w_gate, w_up, w_down):
    rows, feat = tokens.shape
    unit = w_gate.shape[1]
    cap = 3 * rows // (nx * nz)
    half, piece = 4 * cap, 2 * cap
    vm = pltpu.VMEM
    scratch = [
        vm((ny, 2 * feat, 2 * unit), BF16),
        vm((ny, unit, 2 * feat), BF16),
        vm((nz, 2 * cap, feat), BF16),
        vm((nz, 2 * cap, feat), BF16),
        vm((NC, piece, feat), BF16),
        vm((NC, ny, 2 * half, 2 * feat), BF16),
        vm((2 * half, 2 * unit), F32),
        vm((NC, ny, 2 * half, 2 * feat), BF16),
        vm((NC, ny, 2 * half, feat), BF16),
        vm((NC, ny, piece, feat), BF16),
        vm((NC, ny, piece, feat), BF16),
    ]
    scratch += [vm((NC, 2 * half, feat), BF16)] * 6
    scratch += [
        vm((NC, piece, feat), F32),
        vm((NC, half, feat), BF16),
        vm((NC, half, feat), BF16),
        vm((len(PAIRS), piece, feat), F32),
        vm((NC, piece, feat), BF16),
        vm((len(PAIRS), piece, feat), BF16),
        vm((nz, 2 * cap, feat), BF16),
        vm((nz, 2 * cap, feat), BF16),
        vm((rows, feat), BF16),
        vm((rows, nz * 2 * cap), BF16),
        pltpu.SemaphoreType.DMA,
        pltpu.SemaphoreType.DMA((2,)),
        pltpu.SemaphoreType.DMA((SEMS[0],)),
        pltpu.SemaphoreType.DMA((SEMS[1],)),
    ]
    in_vmem = pl.BlockSpec(memory_space=pltpu.VMEM)
    in_hbm = pl.BlockSpec(memory_space=pl.ANY)
    return pl.pallas_call(
        functools.partial(kernel, (nx, ny, nz, cap, feat)),
        out_shape=jax.ShapeDtypeStruct((rows, feat), BF16),
        in_specs=[in_hbm] + [in_vmem] * 2 + [in_hbm] * 3,
        out_specs=in_vmem,
        scratch_shapes=scratch,
        compiler_params=pltpu.CompilerParams(
            collective_id=0, has_side_effects=True, vmem_limit_bytes=60 * 1024 * 1024
        ),
    )(tokens, routes.reshape(1, rows), router_gate.reshape(1, rows), w_gate, w_up, w_down)


def solution(mesh):
    nx, ny = 4, mesh.shape["etp"] // 2
    nz = mesh.shape["ep"] // nx
    return jax.shard_map(
        functools.partial(on_device, nx, ny, nz),
        mesh=mesh,
        in_specs=(
            P("ep", "etp"),
            P("ep", None),
            P("ep", None),
            P(None, ("ep", "etp")),
            P(None, ("ep", "etp")),
            P(("ep", "etp"), None),
        ),
        out_specs=P("ep", "etp"),
        check_vma=False,
    )
```

time: 92.7 us -> 83.3 us (0.90); the launches traced: 92.6 us -> 82.3 us
  Pallas kernels: 90.9 us -> 80.5 us
    pallas_call x1, Pallas kernels: 90.9 us -> 80.5 us  [on_device(): pl.pallas_call(functools.partial(kernel, (nx, ny, nz, cap, feat)), out_sh...]
where the time goes in v3:
time: 83.3 us; the launch traced here: 82.3 us
  Pallas kernels  80.5 us (97%)
  local copies, waits for them, and re-layouts  1.73 us (2%)
    pallas_call x1, Pallas kernels, on_device(): pl.pallas_call(functools.partial(kernel, (nx, ny, nz, cap, feat)), out_sh...  80.5 us
    unnamed x1, local copies, waits for them, and re-layouts  1.73 us

profile of v3, /device:TPU:32, one launch (start us, length us, event | category | flops | bytes accessed | tf_op | source)
XLA Modules:
  0.0 82.3 jit_solution(13411118598196222953)
XLA Ops:
  0.0 80.5 %shard_map.64 = bf16[256,640]{1,0:T(8,128)(2,1)} custom-call(bf16[256,640]{1,0:T(8,128)(2,1)} %tokens.1, s32[1,256]{1,0:T(1,128)} %bitcast.2, bf16[1,256]{1,0:T(2,128)(2,1)} %bitcast.3, bf16[5120,256]{1,0:T(8,128)(2,1)} %w_gate.1, bf16[5120,256]{1,0:T(8,128)(2,1)} %w_up.1, bf16[256,5120]{1,0:T(8,128)(2,1)} %w_down.1), custom_call_target="tpu_custom_call" | custom-call | tf_op jit(solution)/shard_map/pallas_call | solution.py:484
  80.5 1.7 %copy.8 = bf16[256,640]{1,0:T(8,128)(2,1)} copy(bf16[256,640]{1,0:T(8,128)(2,1)} %shard_map.64) | data formatting | bytes 655360

commit v4 on v3

--- a/solution.py
+++ b/solution.py
@@ -21,37 +21,36 @@
     (3, 32, 48),
 )
 WIDE_IN = (0, 0, 0, 0, 0, 0)
-WIDE_OUT = (0, 0, 0, 0, 0, 0)
+WIDE_OUT = (0, 0, 0, 0, 1, 0)
 STRAIGHT_IN = (0, 0, 0, 0, 0, 0)
 STRAIGHT_OUT = (0, 0, 0, 0, 0, 0)
 FLIP = (0, 1, 0, 1, 0, 1)
 NC = len(CHUNKS)
-SEMS = (49, 102)
+SEMS = (49, 103)
 Z_ORDER = (1, 7, 6, 2, 3, 5, 4)
 
 
 ORDER = (
-    ("d1", 0), ("d2", 0), ("d3", 0), ("d1", 1), ("d6", 0, 0), ("d4d", 0), ("d4u", 0), ("d4a", 0),
-    ("d2", 1), ("d1", 5), ("d1", 4), ("d3", 1), ("d5", 0), ("d2", 5), ("d4u", 1), ("d3", 5),
-    ("d2", 4), ("d3", 4), ("d1", 2), ("d4d", 5), ("d6", 0, 1), ("d4a", 1), ("d4a", 5), ("d6", 0, 3),
-    ("d6", 5, 0), ("d4d", 1), ("d6", 0, 2), ("d4u", 4), ("d2", 2), ("d1", 3), ("c", 0),
-    ("d6", 1, 0), ("d5", 5), ("d4u", 5), ("d5", 1), ("d6", 1, 1), ("d6", 1, 3), ("d6", 4, 0),
-    ("d4a", 4), ("d6", 5, 1), ("d4d", 4), ("d3", 2), ("d6", 4, 3), ("d6", 2, 0), ("d2", 3),
-    ("d6", 5, 3), ("d6", 5, 2), ("d3", 3), ("d4d", 2), ("d4u", 2), ("d6", 1, 2), ("d5", 4),
-    ("c", 5), ("d4a", 2), ("e", 5, 1), ("d4d", 3), ("c", 1), ("d4a", 3), ("d4u", 3), ("d6", 4, 2),
-    ("gC", 5), ("d6", 4, 1), ("sC1", 5), ("gC", 0), ("d5", 2), ("e", 1, 2), ("c", 4), ("d5", 3),
-    ("e", 5, 2), ("d6", 3, 0), ("sC1", 0), ("gC", 1), ("e", 5, 0), ("d6", 2, 3), ("d6", 2, 1),
-    ("d6", 3, 3), ("gC", 4), ("e", 4, 2), ("d6", 2, 2), ("sC1", 4), ("e", 4, 3), ("e", 1, 3),
-    ("sC2", 5), ("e", 5, 3), ("gAB", 1), ("c", 2), ("d6", 3, 2), ("gAB", 5), ("sAB1", 5),
-    ("e", 2, 2), ("e", 0, 2), ("e", 4, 1), ("e", 2, 1), ("d6", 3, 1), ("sC1", 2), ("gC", 2),
-    ("gAB", 4), ("e", 0, 3), ("sAB1", 4), ("c", 3), ("gAB", 2), ("sC2", 4), ("sAB2", 5),
-    ("e", 3, 2), ("e", 4, 0), ("e", 2, 3), ("rC", 5), ("gC", 3), ("sC1", 3), ("e", 3, 1),
-    ("e", 3, 3), ("sC2", 2), ("gAB", 0), ("e", 2, 0), ("sAB2", 4), ("gAB", 3), ("sAB2", 2),
-    ("rAB", 5), ("e", 1, 1), ("sAB1", 2), ("rC", 4), ("sC2", 3), ("r4", 5), ("rAB", 4), ("sAB2", 3),
-    ("e", 3, 0), ("sAB1", 3), ("sC2", 0), ("sC1", 1), ("rC", 2), ("sAB1", 1), ("sC2", 1),
-    ("rAB", 2), ("r4", 4), ("e", 0, 0), ("r5", 4), ("sAB2", 1), ("r5", 5), ("e", 0, 1), ("e", 1, 0),
-    ("rC", 3), ("rC", 0), ("rAB", 3), ("r4", 2), ("r5", 2), ("sAB2", 0), ("sAB1", 0), ("r4", 3),
-    ("rAB", 1), ("rC", 1), ("r5", 3), ("rAB", 0), ("r4", 1), ("r4", 0), ("r5", 0), ("r5", 1),
+    ("d1", 0), ("d2", 0), ("d3", 0), ("d1", 1), ("d4u", 0), ("d4d", 0), ("d4a", 0), ("d2", 1),
+    ("d1", 5), ("d1", 4), ("d3", 1), ("d5", 0), ("d2", 5), ("d6", 0, 3), ("d6", 0, 0), ("d6", 0, 1),
+    ("d6", 1, 0), ("d4u", 1), ("d3", 5), ("d2", 4), ("d3", 4), ("d1", 2), ("d6", 5, 0), ("d4u", 5),
+    ("d4a", 5), ("d4d", 5), ("d4u", 4), ("d6", 0, 2), ("d4d", 4), ("d4a", 4), ("d2", 2),
+    ("d6", 5, 1), ("d3", 2), ("d1", 3), ("c", 0), ("d5", 4), ("d6", 4, 3), ("d5", 5), ("d6", 4, 0),
+    ("d4u", 2), ("d2", 3), ("d4d", 2), ("d6", 4, 1), ("d6", 4, 2), ("d4a", 2), ("d3", 3),
+    ("d4a", 1), ("d4d", 1), ("c", 4), ("sC1", 0), ("d4d", 3), ("d6", 2, 3), ("gC", 4), ("d6", 5, 2),
+    ("d5", 2), ("sAB1", 4), ("e", 0, 2), ("d6", 5, 3), ("d4u", 3), ("e", 0, 1), ("d6", 2, 0),
+    ("d6", 1, 1), ("d4a", 3), ("sC1", 4), ("c", 5), ("gAB", 4), ("d6", 2, 2), ("d6", 2, 1),
+    ("gC", 5), ("e", 5, 2), ("d6", 3, 1), ("e", 5, 1), ("gAB", 0), ("gC", 0), ("d5", 3), ("d5", 1),
+    ("c", 2), ("sC1", 5), ("d6", 3, 3), ("e", 5, 3), ("gC", 2), ("e", 2, 2), ("sC2", 4), ("sC1", 2),
+    ("gAB", 5), ("d6", 3, 2), ("d6", 3, 0), ("e", 2, 3), ("e", 5, 0), ("sC2", 5), ("e", 2, 1),
+    ("d6", 1, 3), ("sAB2", 4), ("c", 3), ("sC2", 2), ("gAB", 2), ("sAB1", 5), ("e", 3, 2),
+    ("rC", 5), ("sAB1", 2), ("d6", 1, 2), ("rC", 4), ("gC", 3), ("e", 3, 3), ("e", 3, 1),
+    ("sAB2", 5), ("c", 1), ("gAB", 3), ("e", 2, 0), ("sAB2", 2), ("sC1", 3), ("rAB", 4),
+    ("e", 1, 2), ("r4", 4), ("rC", 2), ("e", 0, 3), ("rAB", 5), ("sC2", 0), ("gC", 1), ("r4", 5),
+    ("sC2", 3), ("sAB1", 3), ("e", 3, 0), ("sAB2", 3), ("rAB", 2), ("e", 1, 1), ("e", 1, 3),
+    ("gAB", 1), ("sAB2", 0), ("rC", 3), ("sC1", 1), ("e", 1, 0), ("r4", 2), ("sC2", 1), ("sAB1", 0),
+    ("rC", 0), ("e", 0, 0), ("rAB", 3), ("sAB1", 1), ("sAB2", 1), ("r4", 3), ("rC", 1), ("rAB", 0),
+    ("rAB", 1), ("r4", 0), ("r4", 1),
 )
 
 BACK = {"up": "dn", "dn": "up", "two": "two", "core": "core", "near": "near", "cross": "cross"}
@@ -60,9 +59,10 @@
 def kernel(sizes, tokens, routes, gate, w_gate, w_up, w_down, out,
            w_gu, w_dn, outgo, zrecv, cross, xs, acc, parts, crecv, xb_out, xb_in,
            ring2, ring2_in, ring_up, ring_up_in, ring_dn, ring_dn_in,
-           own, xn_out, xn_in, fin, fin_x, xc_in, rets, retr, tok, slots_t,
+           own, xn_out, xn_in, fin, fin_x, ret_own, ret_x, retr, tok, slots_t,
            t_sem, w_sem, send_sem, recv_sem):
     nx, ny, nz, cap, feat = sizes
+    tall = -(-cap // 16) * 16
     ep = lax.axis_index("ep")
     etp = lax.axis_index("etp")
     z, x = ep // nx, ep % nx
@@ -83,7 +83,7 @@
     peers = [to[1] for to in (y_up, y_dn, core, x_near, x_cross)]
     if any(STRAIGHT_IN + STRAIGHT_OUT):
         peers.append(y_two[1])
-    peers += [at((z + j) % nz, x, y, c) for j in range(1, nz)]
+    peers += [at((z + j) % nz, xx, y, c) for j in range(1, nz) for xx in (x, nx - 1 - x)]
     for peer in peers:
         pl.semaphore_signal(barrier, inc=1, device_id=peer, device_id_type=MESH)
 
@@ -158,7 +158,10 @@
                 pltpu.make_async_copy(source, target, w_sem.at[sem]).start()
     loads = [pltpu.make_async_copy(w, w, w_sem.at[i]) for i, w in enumerate((w_gu, w_dn))]
 
-    slots_t[...] = (chosen * gate[...].astype(F32)).T.astype(BF16)
+    back_slot = unit_of * (2 * tall) + jnp.where(other, tall, 0) + rank
+    back_place = lax.broadcasted_iota(jnp.int32, (nz * 2 * tall, rows), 0)
+    weighted = jnp.where(back_slot == back_place, gate[...].astype(F32), 0.0)
+    slots_t[...] = weighted.T.astype(BF16)
 
     MINE, THEIRS = pl.ds(0, feat), pl.ds(feat, feat)
     n_of = [hi - lo for _, lo, hi in CHUNKS]
@@ -403,42 +406,45 @@
         if WIDE_OUT[k]:
             wait(k, "xnback")
             crossing = crossing + xn_in[k, B(k)].astype(F32)
-        fin_x[k, A(k)] = crossing.astype(BF16)
-        copies[k]["xcback"] = send(
-            fin_x.at[k, A(k)], xc_in.at[pair, pl.ds(lo, hi - lo)], x_cross
-        )
+        fin_x[pair, lo:hi] = crossing
         own[k, A(k)] = chip_sum(k, 0, A(k)) + neighbours(k, A(k))
+        for j, first, last in ended(k):
+            ret_x[j] = tall_block(fin_x[pair, first:last])
+            to = ("z", at((z + j) % nz, nx - 1 - x, y, c)) if j else x_cross
+            z_back.append(send(ret_x.at[j], retr.at[j, pl.ds(tall, tall)], to))
+
+    def tall_block(block):
+        return jnp.concatenate([block, jnp.zeros((tall - cap, feat), F32)], axis=0).astype(BF16)
+
+    def ended(k):
+        pair, lo, hi = CHUNKS[k]
+        units = [(j, i * cap, (i + 1) * cap) for i, j in enumerate(PAIRS[pair])]
+        return [unit for unit in units if lo < unit[2] <= hi]
 
     def r4(k):
         pair, lo, hi = CHUNKS[k]
         wait(k, "xnback")
         fin[pair, lo:hi] = own[k, A(k)] + xn_in[k, A(k)].astype(F32)
-
-    def r5(k):
-        wait(k, "xcback")
-        pair, lo, hi = CHUNKS[k]
-        for i, j in enumerate(PAIRS[pair]):
-            first, last = i * cap, (i + 1) * cap
-            if lo < last <= hi:
-                kept, crossed = fin[pair, first:last], xc_in[pair, first:last].astype(F32)
-                block = jnp.concatenate([kept, crossed], axis=0).astype(BF16)
-                if j:
-                    rets[j] = block
-                    z_back[j] = send(rets.at[j], retr.at[j], ("z", at((z + j) % nz, x, y, c)))
-                else:
-                    retr[j] = block
-
-    z_back = {}
+        for j, first, last in ended(k):
+            block = tall_block(fin[pair, first:last])
+            if j:
+                ret_own[j] = block
+                to = ("z", at((z + j) % nz, x, y, c))
+                z_back.append(send(ret_own.at[j], retr.at[j, pl.ds(0, tall)], to))
+            else:
+                retr[0, :tall] = block
+
+    z_back = []
     STAGES = dict(
         d1=d1, d2=d2, d3=d3, d4u=d4u, d4d=d4d, d4a=d4a, d5=d5, d6=d6, c=compute, e=e, gC=gC, gAB=gAB,
-        sC1=sC1, sAB1=sAB1, sAB2=sAB2, sC2=sC2, rC=rC, rAB=rAB, r4=r4, r5=r5,
+        sC1=sC1, sAB1=sAB1, sAB2=sAB2, sC2=sC2, rC=rC, rAB=rAB, r4=r4,
     )
     for name, *where in ORDER:
         STAGES[name](*where)
 
-    for j in range(1, nz):
-        finish(z_back[j])
-    back = retr[...].reshape(nz * 2 * cap, feat)
+    for flight in z_back:
+        finish(flight)
+    back = retr[...].reshape(nz * 2 * tall, feat)
     merged = jnp.dot(slots_t[...], back, preferred_element_type=F32)
     out[...] = merged.astype(BF16)
 
@@ -447,7 +453,7 @@
     rows, feat = tokens.shape
     unit = w_gate.shape[1]
     cap = 3 * rows // (nx * nz)
-    half, piece = 4 * cap, 2 * cap
+    half, piece, tall = 4 * cap, 2 * cap, -(-cap // 16) * 16
     vm = pltpu.VMEM
     scratch = [
         vm((ny, 2 * feat, 2 * unit), BF16),
@@ -468,12 +474,12 @@
         vm((NC, half, feat), BF16),
         vm((NC, half, feat), BF16),
         vm((len(PAIRS), piece, feat), F32),
-        vm((NC, piece, feat), BF16),
-        vm((len(PAIRS), piece, feat), BF16),
-        vm((nz, 2 * cap, feat), BF16),
-        vm((nz, 2 * cap, feat), BF16),
+        vm((len(PAIRS), piece, feat), F32),
+        vm((nz, tall, feat), BF16),
+        vm((nz, tall, feat), BF16),
+        vm((nz, 2 * tall, feat), BF16),
         vm((rows, feat), BF16),
-        vm((rows, nz * 2 * cap), BF16),
+        vm((rows, nz * 2 * tall), BF16),
         pltpu.SemaphoreType.DMA,
         pltpu.SemaphoreType.DMA((2,)),
         pltpu.SemaphoreType.DMA((SEMS[0],)),

time: 83.3 us -> 81.6 us (0.980)
  Pallas kernels: 80.5 us -> 78.7 us
    pallas_call x1, Pallas kernels: 80.5 us -> 78.7 us  [on_device(): pl.pallas_call(functools.partial(kernel, (nx, ny, nz, cap, feat)), out_sh...]
where the time goes in v4:
time: 81.6 us; the launch traced here: 80.5 us
  Pallas kernels  78.7 us (96%)
  local copies, waits for them, and re-layouts  1.73 us (2%)
    pallas_call x1, Pallas kernels, on_device(): pl.pallas_call(functools.partial(kernel, (nx, ny, nz, cap, feat)), out_sh...  78.7 us
    unnamed x1, local copies, waits for them, and re-layouts  1.73 us

profile of v4, /device:TPU:32, one launch (start us, length us, event | category | flops | bytes accessed | tf_op | source)
XLA Modules:
  0.0 80.5 jit_solution(4239476147696193682)
XLA Ops:
  0.0 78.7 %shard_map.64 = bf16[256,640]{1,0:T(8,128)(2,1)} custom-call(bf16[256,640]{1,0:T(8,128)(2,1)} %tokens.1, s32[1,256]{1,0:T(1,128)} %bitcast.2, bf16[1,256]{1,0:T(2,128)(2,1)} %bitcast.3, bf16[5120,256]{1,0:T(8,128)(2,1)} %w_gate.1, bf16[5120,256]{1,0:T(8,128)(2,1)} %w_up.1, bf16[256,5120]{1,0:T(8,128)(2,1)} %w_down.1), custom_call_target="tpu_custom_call" | custom-call | tf_op jit(solution)/shard_map/pallas_call | solution.py:490
  78.7 1.7 %copy.8 = bf16[256,640]{1,0:T(8,128)(2,1)} copy(bf16[256,640]{1,0:T(8,128)(2,1)} %shard_map.64) | data formatting | bytes 655360

commit v5 on v4

--- a/solution.py
+++ b/solution.py
@@ -16,41 +16,46 @@
     (0, 0, 16),
     (0, 16, 48),
     (1, 0, 48),
-    (2, 0, 48),
+    (2, 0, 32),
+    (2, 32, 48),
     (3, 0, 32),
     (3, 32, 48),
 )
-WIDE_IN = (0, 0, 0, 0, 0, 0)
-WIDE_OUT = (0, 0, 0, 0, 1, 0)
-STRAIGHT_IN = (0, 0, 0, 0, 0, 0)
-STRAIGHT_OUT = (0, 0, 0, 0, 0, 0)
-FLIP = (0, 1, 0, 1, 0, 1)
+WIDE_IN = (0, 0, 0, 0, 0, 0, 0)
+WIDE_OUT = (0, 0, 0, 0, 0, 1, 0)
+STRAIGHT_IN = (0, 0, 0, 0, 0, 0, 0)
+STRAIGHT_OUT = (0, 0, 0, 0, 0, 0, 0)
+FLIP = (0, 1, 0, 1, 0, 1, 0)
 NC = len(CHUNKS)
-SEMS = (49, 103)
+SEMS = (52, 106)
 Z_ORDER = (1, 7, 6, 2, 3, 5, 4)
 
 
 ORDER = (
-    ("d1", 0), ("d2", 0), ("d3", 0), ("d1", 1), ("d4u", 0), ("d4d", 0), ("d4a", 0), ("d2", 1),
-    ("d1", 5), ("d1", 4), ("d3", 1), ("d5", 0), ("d2", 5), ("d6", 0, 3), ("d6", 0, 0), ("d6", 0, 1),
-    ("d6", 1, 0), ("d4u", 1), ("d3", 5), ("d2", 4), ("d3", 4), ("d1", 2), ("d6", 5, 0), ("d4u", 5),
-    ("d4a", 5), ("d4d", 5), ("d4u", 4), ("d6", 0, 2), ("d4d", 4), ("d4a", 4), ("d2", 2),
-    ("d6", 5, 1), ("d3", 2), ("d1", 3), ("c", 0), ("d5", 4), ("d6", 4, 3), ("d5", 5), ("d6", 4, 0),
-    ("d4u", 2), ("d2", 3), ("d4d", 2), ("d6", 4, 1), ("d6", 4, 2), ("d4a", 2), ("d3", 3),
-    ("d4a", 1), ("d4d", 1), ("c", 4), ("sC1", 0), ("d4d", 3), ("d6", 2, 3), ("gC", 4), ("d6", 5, 2),
-    ("d5", 2), ("sAB1", 4), ("e", 0, 2), ("d6", 5, 3), ("d4u", 3), ("e", 0, 1), ("d6", 2, 0),
-    ("d6", 1, 1), ("d4a", 3), ("sC1", 4), ("c", 5), ("gAB", 4), ("d6", 2, 2), ("d6", 2, 1),
-    ("gC", 5), ("e", 5, 2), ("d6", 3, 1), ("e", 5, 1), ("gAB", 0), ("gC", 0), ("d5", 3), ("d5", 1),
-    ("c", 2), ("sC1", 5), ("d6", 3, 3), ("e", 5, 3), ("gC", 2), ("e", 2, 2), ("sC2", 4), ("sC1", 2),
-    ("gAB", 5), ("d6", 3, 2), ("d6", 3, 0), ("e", 2, 3), ("e", 5, 0), ("sC2", 5), ("e", 2, 1),
-    ("d6", 1, 3), ("sAB2", 4), ("c", 3), ("sC2", 2), ("gAB", 2), ("sAB1", 5), ("e", 3, 2),
-    ("rC", 5), ("sAB1", 2), ("d6", 1, 2), ("rC", 4), ("gC", 3), ("e", 3, 3), ("e", 3, 1),
-    ("sAB2", 5), ("c", 1), ("gAB", 3), ("e", 2, 0), ("sAB2", 2), ("sC1", 3), ("rAB", 4),
-    ("e", 1, 2), ("r4", 4), ("rC", 2), ("e", 0, 3), ("rAB", 5), ("sC2", 0), ("gC", 1), ("r4", 5),
-    ("sC2", 3), ("sAB1", 3), ("e", 3, 0), ("sAB2", 3), ("rAB", 2), ("e", 1, 1), ("e", 1, 3),
-    ("gAB", 1), ("sAB2", 0), ("rC", 3), ("sC1", 1), ("e", 1, 0), ("r4", 2), ("sC2", 1), ("sAB1", 0),
-    ("rC", 0), ("e", 0, 0), ("rAB", 3), ("sAB1", 1), ("sAB2", 1), ("r4", 3), ("rC", 1), ("rAB", 0),
-    ("rAB", 1), ("r4", 0), ("r4", 1),
+    ("d1", 0), ("d2", 0), ("d3", 0), ("d1", 1), ("d6", 0, 0), ("d4d", 0), ("d4u", 0), ("d4a", 0),
+    ("d2", 1), ("d3", 1), ("d1", 5), ("d5", 0), ("d1", 6), ("d4d", 1), ("d2", 5), ("d4u", 1),
+    ("d3", 5), ("d2", 6), ("d6", 1, 0), ("d4a", 1), ("d3", 6), ("d6", 0, 3), ("d1", 2), ("d4u", 5),
+    ("d4u", 6), ("d6", 6, 0), ("d4d", 5), ("d6", 1, 3), ("d6", 0, 2), ("d6", 0, 1), ("d4a", 5),
+    ("d6", 1, 1), ("d5", 1), ("d4a", 6), ("d2", 2), ("d3", 2), ("d1", 3), ("d1", 4), ("ca", 0),
+    ("d6", 5, 3), ("d6", 5, 1), ("ca", 1), ("d5", 5), ("d6", 1, 2), ("d4d", 6), ("d5", 6),
+    ("d6", 5, 0), ("d6", 6, 3), ("d4u", 2), ("d2", 3), ("c", 1), ("d4d", 2), ("d4a", 2), ("d2", 4),
+    ("d3", 3), ("e", 1, 1), ("d6", 5, 2), ("d3", 4), ("ca", 5), ("gC", 1), ("d6", 6, 2),
+    ("d6", 2, 0), ("d6", 6, 1), ("c", 5), ("d4d", 3), ("ca", 6), ("gC", 5), ("gAB", 5), ("d5", 2),
+    ("d4d", 4), ("d6", 2, 3), ("c", 6), ("d6", 2, 1), ("d4u", 3), ("d4a", 3), ("d6", 3, 0),
+    ("d4u", 4), ("e", 1, 2), ("gC", 6), ("e", 6, 2), ("sC1", 5), ("sAB1", 5), ("ca", 2),
+    ("d6", 2, 2), ("e", 6, 1), ("d4a", 4), ("sC1", 1), ("e", 6, 3), ("d6", 3, 1), ("sC1", 6),
+    ("c", 2), ("d5", 3), ("sC2", 6), ("sC2", 5), ("sAB2", 5), ("d6", 4, 1), ("d6", 3, 3),
+    ("e", 2, 2), ("c", 0), ("gAB", 6), ("d5", 4), ("gC", 2), ("gAB", 1), ("e", 2, 3), ("sC1", 2),
+    ("e", 2, 1), ("ca", 3), ("d6", 4, 3), ("sAB1", 6), ("d6", 3, 2), ("d6", 4, 0), ("rC", 5),
+    ("gAB", 2), ("d6", 4, 2), ("c", 3), ("rC", 6), ("sC2", 1), ("sC2", 2), ("sAB1", 2), ("sAB2", 6),
+    ("e", 3, 2), ("e", 6, 0), ("e", 2, 0), ("ca", 4), ("gC", 3), ("c", 4), ("sAB2", 2), ("e", 4, 2),
+    ("e", 3, 1), ("e", 4, 3), ("rAB", 5), ("gC", 4), ("gAB", 3), ("rAB", 6), ("sC1", 3),
+    ("e", 3, 3), ("e", 4, 1), ("r4", 5), ("r4", 6), ("rC", 2), ("sC1", 4), ("gAB", 4), ("e", 0, 2),
+    ("e", 1, 3), ("e", 3, 0), ("gC", 0), ("sC2", 4), ("sC2", 3), ("e", 0, 1), ("sAB1", 4),
+    ("sAB1", 3), ("e", 4, 0), ("rAB", 2), ("sAB2", 3), ("e", 0, 3), ("sAB2", 4), ("rC", 3),
+    ("sC2", 0), ("gAB", 0), ("r4", 2), ("sC1", 0), ("sAB2", 1), ("rC", 4), ("e", 0, 0), ("sAB1", 1),
+    ("e", 1, 0), ("rAB", 3), ("rAB", 4), ("rC", 1), ("sAB1", 0), ("sAB2", 0), ("rC", 0), ("r4", 3),
+    ("r4", 4), ("rAB", 0), ("rAB", 1), ("r4", 0), ("r4", 1),
 )
 
 BACK = {"up": "dn", "dn": "up", "two": "two", "core": "core", "near": "near", "cross": "cross"}
@@ -175,6 +180,9 @@
     def AB(k):
         return pl.ds(0, 2 * n_of[k])
 
+    def ALL(k):
+        return pl.ds(0, 4 * n_of[k])
+
     def NEAR_A(k):
         return pl.ds(2 * n_of[k], n_of[k])
 
@@ -291,20 +299,29 @@
             mine = xs.at[k, r, NEAR_B(k), MINE]
             copies[k]["cB", r] = send(mine, xs.at[k, r, NEAR_B(k), THEIRS], core)
 
+    def gate_up(k, r):
+        if r == 0:
+            wait(k, "c0", "c0C")
+        else:
+            wait(k, ("c", r))
+        if not WIDE_IN[k]:
+            wait(k, ("cB", r))
+        return jnp.dot(xs[k, r, ALL(k), :], w_gu[r], preferred_element_type=F32)
+
+    def early(k):
+        while loads:
+            loads.pop().wait()
+        acc[k, ALL(k), :] = gate_up(k, 0)
+        for r in (1, 3):
+            acc[k, ALL(k), :] += gate_up(k, r)
+
     def compute(k):
         co = copies[k]
-        while loads:
-            loads.pop().wait()
-        whole = pl.ds(0, 4 * n_of[k])
-        for i, r in enumerate((0, 1, 3, 2)):
-            wait(k, *(("c0", "c0C") if r == 0 else (("c", r),)))
-            if not WIDE_IN[k]:
-                wait(k, ("cB", r))
-            pre = jnp.dot(xs[k, r, whole, :], w_gu[r], preferred_element_type=F32)
-            acc[whole, :] = pre if i == 0 else acc[whole, :] + pre
+        whole = ALL(k)
+        both = acc[k, whole, :] + gate_up(k, 2)
         unit = w_gate.shape[1]
-        pre = acc[whole, :unit]
-        hidden = (pre / (1.0 + jnp.exp(-pre)) * acc[whole, unit:]).astype(BF16)
+        pre = both[:, :unit]
+        hidden = (pre / (1.0 + jnp.exp(-pre)) * both[:, unit:]).astype(BF16)
         for r in (2, 1, 3, 0):
             parts[k, r, whole, :] = jnp.dot(
                 hidden, w_dn[r], preferred_element_type=F32
@@ -436,7 +453,7 @@
 
     z_back = []
     STAGES = dict(
-        d1=d1, d2=d2, d3=d3, d4u=d4u, d4d=d4d, d4a=d4a, d5=d5, d6=d6, c=compute, e=e, gC=gC, gAB=gAB,
+        d1=d1, d2=d2, d3=d3, d4u=d4u, d4d=d4d, d4a=d4a, d5=d5, d6=d6, ca=early, c=compute, e=e, gC=gC, gAB=gAB,
         sC1=sC1, sAB1=sAB1, sAB2=sAB2, sC2=sC2, rC=rC, rAB=rAB, r4=r4,
     )
     for name, *where in ORDER:
@@ -462,7 +479,7 @@
         vm((nz, 2 * cap, feat), BF16),
         vm((NC, piece, feat), BF16),
         vm((NC, ny, 2 * half, 2 * feat), BF16),
-        vm((2 * half, 2 * unit), F32),
+        vm((NC, 2 * half, 2 * unit), F32),
         vm((NC, ny, 2 * half, 2 * feat), BF16),
         vm((NC, ny, 2 * half, feat), BF16),
         vm((NC, ny, piece, feat), BF16),

time: 81.6 us -> 80.7 us (0.989)
  Pallas kernels: 78.7 us -> 77.7 us
    pallas_call x1, Pallas kernels: 78.7 us -> 77.7 us  [on_device(): pl.pallas_call(functools.partial(kernel, (nx, ny, nz, cap, feat)), out_sh...]
where the time goes in v5:
time: 80.7 us; the launch traced here: 79.4 us
  Pallas kernels  77.7 us (96%)
  local copies, waits for them, and re-layouts  1.73 us (2%)
    pallas_call x1, Pallas kernels, on_device(): pl.pallas_call(functools.partial(kernel, (nx, ny, nz, cap, feat)), out_sh...  77.7 us
    unnamed x1, local copies, waits for them, and re-layouts  1.73 us

profile of v5, /device:TPU:32, one launch (start us, length us, event | category | flops | bytes accessed | tf_op | source)
XLA Modules:
  0.0 79.4 jit_solution(8330770769974860262)
XLA Ops:
  0.0 77.7 %shard_map.64 = bf16[256,640]{1,0:T(8,128)(2,1)} custom-call(bf16[256,640]{1,0:T(8,128)(2,1)} %tokens.1, s32[1,256]{1,0:T(1,128)} %bitcast.2, bf16[1,256]{1,0:T(2,128)(2,1)} %bitcast.3, bf16[5120,256]{1,0:T(8,128)(2,1)} %w_gate.1, bf16[5120,256]{1,0:T(8,128)(2,1)} %w_up.1, bf16[256,5120]{1,0:T(8,128)(2,1)} %w_down.1), custom_call_target="tpu_custom_call" | custom-call | tf_op jit(solution)/shard_map/pallas_call | solution.py:507
  77.7 1.7 %copy.8 = bf16[256,640]{1,0:T(8,128)(2,1)} copy(bf16[256,640]{1,0:T(8,128)(2,1)} %shard_map.64) | data formatting | bytes 655360
